TPU v7x, 32 devices: a whole 2x2x4 slice. The times are simulated.
32 devices in a mesh: dp: 2 (over x), expert: 16 (over z, y, core).
Axes of the slice: x: 2, y: 2, z: 4, core: 2. Of those that a mesh axis runs over, the one named last changes fastest.
Arguments:
- tokens: bfloat16 [4096, 4096], P('expert', 'dp'), may hold values from -6 to 6
- out_grad: bfloat16 [4096, 4096], P('expert', 'dp'), may hold values from -3 to 3
- expert_ids: int32 [4096, 2], P('expert'), may hold values from 0 to 15, as said below
- gate_probs: float32 [4096, 2], P('expert'), may hold values from 0.25 to 1
- w_gate: bfloat16 [16, 4096, 1024], P('expert', 'dp'), may hold values from -0.09375 to 0.09375
- w_up: bfloat16 [16, 4096, 1024], P('expert', 'dp'), may hold values from -0.09375 to 0.09375
- w_down: bfloat16 [16, 1024, 4096], P('expert', None, 'dp'), may hold values from -0.1875 to 0.1875
Outputs:
- token_grad: bfloat16 [4096, 4096], P('expert', 'dp')
- grad_w_gate: float32 [16, 4096, 1024], P('expert', 'dp')
- grad_w_up: float32 [16, 4096, 1024], P('expert', 'dp')
- grad_w_down: float32 [16, 1024, 4096], P('expert', None, 'dp')
Inputs may be any that keep to these rules, and one draw needn't show every extreme that they name: `expert_ids`: A token's two ids differ. Among the tokens of one aligned block of 256 tokens no expert is named more than 32 times; 4 experts, the same for every block, are named exactly 32 times in each block.
All inputs are finite; a program needn't handle non-finite values.
Results may differ from a plain program's by a relative error of at most 0.02.
Values may be sent and summed in bfloat16 or wider, within the bound.
A program may use at most 128 MiB of HBM per device.

v0:
```python
import jax
import jax.numpy as jnp
from jax import lax
from jax.sharding import PartitionSpec as P

MOST = 32


contract_rows = (((0,), (0,)), ((), ()))
contract_cols = (((1,), (1,)), ((), ()))


def silu_parts(pre_gate):
    sigmoid_gate = jax.nn.sigmoid(pre_gate)
    return (pre_gate * sigmoid_gate, sigmoid_gate * (1.0 + pre_gate * (1.0 - sigmoid_gate)))


def local_grads(pre_gate, pre_up, grad_act):
    active, slope_gate = silu_parts(pre_gate)
    hidden = (active * pre_up).astype(jnp.bfloat16)
    grad_gate = (grad_act * pre_up * slope_gate).astype(jnp.bfloat16)
    grad_up = (grad_act * active).astype(jnp.bfloat16)
    return (hidden, grad_gate, grad_up)


def shards(tokens, out_grad, expert_ids, gate_probs, w_gate, w_up, w_down):
    tok_rows, slab_width = tokens.shape
    owners = lax.axis_size("expert")
    experts = owners * w_gate.shape[0]
    pick_ids = expert_ids.T.reshape(-1)
    onehot = (pick_ids[:, None] == jnp.arange(experts, dtype=jnp.int32)[None, :]).astype(jnp.int32)
    rank_in = jnp.sum((jnp.cumsum(onehot, axis=0) - 1) * onehot, axis=1)
    slot_of = pick_ids * MOST + rank_in
    placing = (jnp.arange(experts * MOST, dtype=jnp.int32)[:, None] == slot_of[None, :]).astype(
        jnp.bfloat16
    )
    row_pick = jnp.concatenate([tokens, tokens], axis=0)
    grad_pick = jnp.concatenate([out_grad, out_grad], axis=0)
    scaled = (gate_probs.T.reshape(-1)[:, None] * grad_pick.astype(jnp.float32)).astype(
        jnp.bfloat16
    )
    send_tokens = (
        jnp.dot(placing, row_pick, preferred_element_type=jnp.float32)
        .astype(jnp.bfloat16)
        .reshape(experts, MOST, slab_width)
    )
    send_grads = (
        jnp.dot(placing, scaled, preferred_element_type=jnp.float32)
        .astype(jnp.bfloat16)
        .reshape(experts, MOST, slab_width)
    )
    arrived_tokens, arrived_grads = (
        lax.all_to_all(send_tokens, "expert", split_axis=0, concat_axis=0, tiled=True),
        lax.all_to_all(send_grads, "expert", split_axis=0, concat_axis=0, tiled=True),
    )
    flat_tokens = arrived_tokens.reshape(-1, slab_width)
    flat_grads = arrived_grads.reshape(-1, slab_width)
    gate_mat = w_gate[0]
    up_mat = w_up[0]
    down_mat = w_down[0]
    part_gate = jnp.dot(flat_tokens, gate_mat, preferred_element_type=jnp.float32)
    part_up = jnp.dot(flat_tokens, up_mat, preferred_element_type=jnp.float32)
    part_act = lax.dot_general(
        flat_grads, down_mat, contract_cols, preferred_element_type=jnp.float32
    )
    pre_gate, pre_up, grad_act = (
        lax.psum(part_gate.astype(jnp.bfloat16), "dp").astype(jnp.float32),
        lax.psum(part_up.astype(jnp.bfloat16), "dp").astype(jnp.float32),
        lax.psum(part_act.astype(jnp.bfloat16), "dp").astype(jnp.float32),
    )
    hidden, grad_gate, grad_up = local_grads(pre_gate, pre_up, grad_act)
    slot_grad = lax.dot_general(
        grad_gate, gate_mat, contract_cols, preferred_element_type=jnp.float32
    )
    slot_grad = slot_grad + lax.dot_general(
        grad_up, up_mat, contract_cols, preferred_element_type=jnp.float32
    )
    gate_grads = lax.dot_general(
        flat_tokens, grad_gate, contract_rows, preferred_element_type=jnp.float32
    )[None]
    up_grads = lax.dot_general(
        flat_tokens, grad_up, contract_rows, preferred_element_type=jnp.float32
    )[None]
    down_grads = lax.dot_general(
        hidden, flat_grads, contract_rows, preferred_element_type=jnp.float32
    )[None]
    returned = lax.all_to_all(
        slot_grad.reshape(experts, MOST, slab_width).astype(jnp.bfloat16),
        "expert",
        split_axis=0,
        concat_axis=0,
        tiled=True,
    ).astype(jnp.float32)
    flat_back = returned.reshape(experts * MOST, slab_width)
    per_pick = jnp.take(flat_back, slot_of, axis=0)
    token_grad = (per_pick[:tok_rows] + per_pick[tok_rows:]).astype(jnp.bfloat16)
    return (token_grad, gate_grads, up_grads, down_grads)


def solution(mesh):
    in_specs = (
        P("expert", "dp"),
        P("expert", "dp"),
        P("expert", None),
        P("expert", None),
        P("expert", "dp", None),
        P("expert", "dp", None),
        P("expert", None, "dp"),
    )
    out_specs = (
        P("expert", "dp"),
        P("expert", "dp", None),
        P("expert", "dp", None),
        P("expert", None, "dp"),
    )
    return jax.shard_map(shards, mesh=mesh, in_specs=in_specs, out_specs=out_specs, check_vma=False)
```

profile of v0, /device:TPU:0, one launch (start us, length us, event | category | flops | bytes accessed | tf_op | source)
XLA Modules:
  0.0 292.1 jit_solution(15745471083507589220)
XLA Ops:
  7.2 0.7 eq.39
  7.9 0.7 copy.13
  8.6 1.1 reduce-window.6
  10.1 4.2 %convolution_convert_fusion = bf16[512,2048]{1,0:T(8,128)(2,1)} fusion(bf16[256,2048]{1,0:T(8,128)(2,1)} %param.7, s32[512]{0:T(512)S(1)} %get-tuple-element.8), kind=kOutput, calls=%fused_computation.19 | convolution fusion | flops 1079246848 | bytes 3147776 | tf_op jit(solution)/shard_map/dot_general | solution.py:43
  14.2 7.5 %all-to-all-start.1 = ((bf16[16,32,2048]{2,1,0:T(8,128)(2,1)}), bf16[16,32,2048]{2,1,0:T(8,128)(2,1)S(1)}, u32[]{:S(2)}, u32[]{:S(2)}) async-start(bf16[16,32,2048]{2,1,0:T(8,128)(2,1)} %bitcast.76), calls=%async_computation.1 | async-start | bytes 4194304 | tf_op jit(solution)/shard_map/all_to_all | solution.py:53
  21.8 2.7 convolution_convert_fusion.1
  24.5 38.4 %all-to-all-done.1 = bf16[16,32,2048]{2,1,0:T(8,128)(2,1)S(1)} async-done(((bf16[16,32,2048]{2,1,0:T(8,128)(2,1)}), bf16[16,32,2048]{2,1,0:T(8,128)(2,1)S(1)}, u32[]{:S(2)}, u32[]{:S(2)}) %all-to-all-start.1) | async-done | bytes 2097184 | tf_op jit(solution)/shard_map/all_to_all | solution.py:53
  62.9 11.3 %all-to-all-start = ((bf16[16,32,2048]{2,1,0:T(8,128)(2,1)}), bf16[16,32,2048]{2,1,0:T(8,128)(2,1)}, u32[]{:S(2)}, u32[]{:S(2)}) async-start(bf16[16,32,2048]{2,1,0:T(8,128)(2,1)} %bitcast.75), calls=%async_computation | async-start | bytes 4194304 | tf_op jit(solution)/shard_map/all_to_all | solution.py:54
  74.4 5.7 %fusion.35 = bf16[512,1024]{1,0:T(8,128)(2,1)} fusion(bf16[512,2048]{1,0:T(8,128)(2,1)S(1)} %bitcast.70, bf16[1,2048,1024]{2,1,0:T(8,128)(2,1)} %param.11), kind=kOutput, calls=%fused_computation.46 | convolution fusion | flops 2148007936 | bytes 7340032 | tf_op jit(solution)/shard_map/dot_general | solution.py:61
  80.0 3.3 %fusion.32 = bf16[512,1024]{1,0:T(8,128)(2,1)} fusion(bf16[512,2048]{1,0:T(8,128)(2,1)S(1)} %bitcast.71, bf16[1,2048,1024]{2,1,0:T(8,128)(2,1)S(1)} %copy-done.4), kind=kOutput, calls=%fused_computation.45 | convolution fusion | flops 2148007936 | bytes 7340032 | tf_op jit(solution)/shard_map/dot_general | solution.py:62
  83.4 31.9 %all-to-all-done = bf16[16,32,2048]{2,1,0:T(8,128)(2,1)} async-done(((bf16[16,32,2048]{2,1,0:T(8,128)(2,1)}), bf16[16,32,2048]{2,1,0:T(8,128)(2,1)}, u32[]{:S(2)}, u32[]{:S(2)}) %all-to-all-start) | async-done | bytes 2097184 | tf_op jit(solution)/shard_map/all_to_all | solution.py:54
  115.3 6.2 %fusion.29 = bf16[512,1024]{1,0:T(8,128)(2,1)} fusion(bf16[512,2048]{1,0:T(8,128)(2,1)} %bitcast.4, bf16[1,1024,2048]{2,1,0:T(8,128)(2,1)} %param.13), kind=kOutput, calls=%fused_computation.44 | convolution fusion | flops 2148007936 | bytes 7340032 | tf_op jit(solution)/shard_map/dot_general | solution.py:63
  121.5 92.8 %all-reduce.3.cloned.1.call-done = (bf16[512,1024]{1,0:T(8,128)(2,1)}, bf16[512,1024]{1,0:T(8,128)(2,1)}, bf16[512,1024]{1,0:T(8,128)(2,1)}) async-done(((bf16[512,1024]{1,0:T(8,128)(2,1)}, bf16[512,1024]{1,0:T(8,128)(2,1)}, bf16[512,1024]{1,0:T(8,128)(2,1)}), (bf16[512,1024]{1,0:T(8,128)(2,1)}, bf16[512,1024]{1,0:T(8,128)(2,1)}, bf16[512,1024]{1,0:T(8,128)(2,1)})) %all-reduce.3.cloned.1.call-update) | async-done | bytes 3145744 | tf_op jit(solution)/shard_map/psum | solution.py:68
  214.3 6.1 %fusion = f32[512,2048]{1,0:T(8,128)S(1)} fusion(bf16[1,2048,1024]{2,1,0:T(8,128)(2,1)} %param.11, bf16[512,1024]{1,0:T(8,128)(2,1)} %get-tuple-element.4, bf16[512,1024]{1,0:T(8,128)(2,1)} %get-tuple-element.5, bf16[512,1024]{1,0:T(8,128)(2,1)} %get-tuple-element.6), kind=kOutput, calls=%fused_computation.4 | convolution fusion | flops 2154299392 | bytes 11534336 | tf_op jit(solution)/shard_map/dot_general | solution.py:72
  220.5 3.9 %add_convert_fusion = bf16[512,2048]{1,0:T(8,128)(2,1)} fusion(f32[512,2048]{1,0:T(8,128)S(1)} %fusion, bf16[1,2048,1024]{2,1,0:T(8,128)(2,1)S(1)} %copy-done.5, bf16[512,1024]{1,0:T(8,128)(2,1)S(1)} %copy-done.8, bf16[512,1024]{1,0:T(8,128)(2,1)S(1)} %copy-done.10), kind=kOutput, calls=%fused_computation.14 | convolution fusion | flops 2153775104 | bytes 12582912 | tf_op jit(solution)/shard_map/dot_general | solution.py:75
  224.4 5.8 %all-to-all-start.2 = ((bf16[16,32,2048]{2,1,0:T(8,128)(2,1)}), bf16[16,32,2048]{2,1,0:T(8,128)(2,1)S(1)}, u32[]{:S(2)}, u32[]{:S(2)}) async-start(bf16[16,32,2048]{2,1,0:T(8,128)(2,1)} %bitcast.74), calls=%async_computation.2 | async-start | bytes 4194304 | tf_op jit(solution)/shard_map/all_to_all | solution.py:87
  230.3 8.0 %convolution_bitcast_fusion = f32[1,1024,2048]{2,1,0:T(8,128)} fusion(bf16[512,2048]{1,0:T(8,128)(2,1)} %bitcast.4, bf16[512,1024]{1,0:T(8,128)(2,1)S(1)} %copy-done.7, bf16[512,1024]{1,0:T(8,128)(2,1)} %get-tuple-element.6), kind=kOutput, calls=%fused_computation.1 | convolution fusion | flops 2151677952 | bytes 12582912 | tf_op jit(solution)/shard_map/dot_general | solution.py:84
  238.3 5.9 %convolution_bitcast_fusion.1 = f32[1,2048,1024]{2,1,0:T(8,128)} fusion(bf16[512,2048]{1,0:T(8,128)(2,1)S(1)} %bitcast.72, bf16[512,1024]{1,0:T(8,128)(2,1)S(1)} %copy-done.9, bf16[512,1024]{1,0:T(8,128)(2,1)S(1)} %copy-done.11), kind=kOutput, calls=%fused_computation.2 | convolution fusion | flops 2151677952 | bytes 12582912 | tf_op jit(solution)/shard_map/dot_general | solution.py:81
  244.2 6.0 %convolution_bitcast_fusion.2 = f32[1,2048,1024]{2,1,0:T(8,128)} fusion(bf16[512,2048]{1,0:T(8,128)(2,1)S(1)} %bitcast.73, bf16[512,1024]{1,0:T(8,128)(2,1)S(1)} %copy-done.7, bf16[512,1024]{1,0:T(8,128)(2,1)S(1)} %copy-done.9, bf16[512,1024]{1,0:T(8,128)(2,1)S(1)} %copy-done.11), kind=kOutput, calls=%fused_computation.3 | convolution fusion | flops 2154299392 | bytes 13631488 | tf_op jit(solution)/shard_map/dot_general | solution.py:78
  250.2 21.1 %all-to-all-done.2 = bf16[16,32,2048]{2,1,0:T(8,128)(2,1)S(1)} async-done(((bf16[16,32,2048]{2,1,0:T(8,128)(2,1)}), bf16[16,32,2048]{2,1,0:T(8,128)(2,1)S(1)}, u32[]{:S(2)}, u32[]{:S(2)}) %all-to-all-start.2) | async-done | bytes 2097184 | tf_op jit(solution)/shard_map/all_to_all | solution.py:87
  271.3 2.6 bitcast_convert_fusion
  273.9 7.6 %gather_fusion = f32[512,2048]{1,0:T(8,128)} fusion(f32[512,2048]{1,0:T(8,128)} %bitcast_convert_fusion, s32[1024]{0:T(1024)S(1)} %pad_clamp_fusion), kind=kCustom, calls=%fused_computation | custom fusion | bytes 8390656 | tf_op jit(solution)/shard_map/jit(_take)/gather | solution.py:95
  281.5 2.5 broadcast_select_fusion
  284.0 1.2 fusion.21
  (37 shorter events, 0.7 us)
Async XLA Ops:
  14.2 7.5 %copy-start.3 = (f32[256,2]{0,1:T(2,128)S(1)}, f32[256,2]{0,1:T(2,128)}, u32[]{:S(2)}) copy-start(f32[256,2]{0,1:T(2,128)} %param.10) | copy-start | bytes 6148
  14.2 7.5 %copy-start.6 = (bf16[256,2048]{1,0:T(8,128)(2,1)S(1)}, bf16[256,2048]{1,0:T(8,128)(2,1)}, u32[]{:S(2)}) copy-start(bf16[256,2048]{1,0:T(8,128)(2,1)} %param.8) | copy-start | bytes 3145732
  14.2 48.6 %all-to-all-start.1 = ((bf16[16,32,2048]{2,1,0:T(8,128)(2,1)}), bf16[16,32,2048]{2,1,0:T(8,128)(2,1)S(1)}, u32[]{:S(2)}, u32[]{:S(2)}) async-start(bf16[16,32,2048]{2,1,0:T(8,128)(2,1)} %bitcast.76), calls=%async_computation.1 | async-start | bytes 4194304 | tf_op jit(solution)/shard_map/all_to_all | solution.py:53
  62.9 17.2 %copy-start = (bf16[16,32,2048]{2,1,0:T(8,128)(2,1)}, bf16[16,32,2048]{2,1,0:T(8,128)(2,1)S(1)}, u32[]{:S(2)}) copy-start(bf16[16,32,2048]{2,1,0:T(8,128)(2,1)S(1)} %all-to-all-done.1) | copy-start | bytes 6291460
  62.9 52.4 %all-to-all-start = ((bf16[16,32,2048]{2,1,0:T(8,128)(2,1)}), bf16[16,32,2048]{2,1,0:T(8,128)(2,1)}, u32[]{:S(2)}, u32[]{:S(2)}) async-start(bf16[16,32,2048]{2,1,0:T(8,128)(2,1)} %bitcast.75), calls=%async_computation | async-start | bytes 4194304 | tf_op jit(solution)/shard_map/all_to_all | solution.py:54
  74.1 140.2 %all-reduce.3.cloned.1.call-start = ((), (), s32[]{:S(2)}) async-start(), calls=%async_computation.3 | async-start | bytes 6291456 | tf_op jit(solution)/shard_map/psum | solution.py:68
  74.4 5.7 %copy-start.4 = (bf16[1,2048,1024]{2,1,0:T(8,128)(2,1)S(1)}, bf16[1,2048,1024]{2,1,0:T(8,128)(2,1)}, u32[]{:S(2)}) copy-start(bf16[1,2048,1024]{2,1,0:T(8,128)(2,1)} %param.12) | copy-start | bytes 12582916
  214.3 6.2 %copy-start.5 = (bf16[1,2048,1024]{2,1,0:T(8,128)(2,1)S(1)}, bf16[1,2048,1024]{2,1,0:T(8,128)(2,1)}, u32[]{:S(2)}) copy-start(bf16[1,2048,1024]{2,1,0:T(8,128)(2,1)} %param.12) | copy-start | bytes 12582916
  214.3 6.2 %copy-start.8 = (bf16[512,1024]{1,0:T(8,128)(2,1)S(1)}, bf16[512,1024]{1,0:T(8,128)(2,1)}, u32[]{:S(2)}) copy-start(bf16[512,1024]{1,0:T(8,128)(2,1)} %get-tuple-element.5) | copy-start | bytes 3145732
  214.3 6.2 %copy-start.10 = (bf16[512,1024]{1,0:T(8,128)(2,1)S(1)}, bf16[512,1024]{1,0:T(8,128)(2,1)}, u32[]{:S(2)}) copy-start(bf16[512,1024]{1,0:T(8,128)(2,1)} %get-tuple-element.6) | copy-start | bytes 3145732
  224.4 5.8 %copy-start.2 = (s32[256,2]{0,1:T(2,128)S(1)}, s32[256,2]{0,1:T(2,128)}, u32[]{:S(2)}) copy-start(s32[256,2]{0,1:T(2,128)} %param.9) | copy-start | bytes 6148
  224.4 5.8 %copy-start.7 = (bf16[512,1024]{1,0:T(8,128)(2,1)S(1)}, bf16[512,1024]{1,0:T(8,128)(2,1)}, u32[]{:S(2)}) copy-start(bf16[512,1024]{1,0:T(8,128)(2,1)} %get-tuple-element.4) | copy-start | bytes 3145732
  224.4 46.9 %all-to-all-start.2 = ((bf16[16,32,2048]{2,1,0:T(8,128)(2,1)}), bf16[16,32,2048]{2,1,0:T(8,128)(2,1)S(1)}, u32[]{:S(2)}, u32[]{:S(2)}) async-start(bf16[16,32,2048]{2,1,0:T(8,128)(2,1)} %bitcast.74), calls=%async_computation.2 | async-start | bytes 4194304 | tf_op jit(solution)/shard_map/all_to_all | solution.py:87
  230.2 8.0 %copy-start.1 = (bf16[16,32,2048]{2,1,0:T(8,128)(2,1)S(1)}, bf16[16,32,2048]{2,1,0:T(8,128)(2,1)}, u32[]{:S(2)}) copy-start(bf16[16,32,2048]{2,1,0:T(8,128)(2,1)} %copy-done) | copy-start | bytes 6291460
  230.2 8.0 %copy-start.9 = (bf16[512,1024]{1,0:T(8,128)(2,1)S(1)}, bf16[512,1024]{1,0:T(8,128)(2,1)}, u32[]{:S(2)}) copy-start(bf16[512,1024]{1,0:T(8,128)(2,1)} %get-tuple-element.5) | copy-start | bytes 3145732
  230.2 8.0 %copy-start.11 = (bf16[512,1024]{1,0:T(8,128)(2,1)S(1)}, bf16[512,1024]{1,0:T(8,128)(2,1)}, u32[]{:S(2)}) copy-start(bf16[512,1024]{1,0:T(8,128)(2,1)} %get-tuple-element.6) | copy-start | bytes 3145732
Sparse Core Ops, SparseCore 0:
  121.6 92.6 all-reduce.2
where the time goes:
time: 298 us; the launch traced here: 292 us
  waiting for transfers between devices  184 us (62%)
  matrix products  52 us (17%)
  starting transfers between devices  24.8 us (8%)
  between operations  14.2 us (5%)
  local copies, waits for them, and re-layouts  9.28 us (3%)
  other arithmetic  7.68 us (3%)
    psum x1, waiting for transfers between devices, shards(): lax.psum(part_up.astype(jnp.bfloat16), 'dp').astype(jnp.float32)  92.8 us
    all_to_all x1, waiting for transfers between devices, shards(): lax.all_to_all(send_tokens, 'expert', split_axis=0, concat_axis=0, tiled=...  38.4 us
    all_to_all x1, waiting for transfers between devices, shards(): lax.all_to_all(send_grads, 'expert', split_axis=0, concat_axis=0, tiled=T...  31.9 us
    all_to_all x1, waiting for transfers between devices, shards(): lax.all_to_all(slot_grad.reshape(experts, MOST, slab_width).astype(jnp.bf...  21.1 us
    all_to_all x1, starting transfers between devices, shards(): lax.all_to_all(send_grads, 'expert', split_axis=0, concat_axis=0, tiled=T...  11.3 us
    dot_general x1, matrix products, shards(): lax.dot_general(hidden, flat_grads, contract_rows, preferred_element_type...  7.99 us
    gather x1, local copies, waits for them, and re-layouts, shards(): per_pick = jnp.take(flat_back, slot_of, axis=0)  7.62 us
    all_to_all x1, starting transfers between devices, shards(): lax.all_to_all(send_tokens, 'expert', split_axis=0, concat_axis=0, tiled=...  7.52 us
  transfers between devices with their start and end apart: 4, of which 4 were waited for; matrix products, arithmetic and copies ran while one was open for 11% of the time, Pallas kernels for 0%

commit v1 on v0

--- a/solution.py
+++ b/solution.py
@@ -1,6 +1,10 @@
+import functools
+
 import jax
 import jax.numpy as jnp
 from jax import lax
+from jax.experimental import pallas as pl
+from jax.experimental.pallas import tpu as pltpu
 from jax.sharding import PartitionSpec as P
 
 MOST = 32
@@ -97,6 +101,330 @@
     return (token_grad, gate_grads, up_grads, down_grads)
 
 
+GROUP = 4
+TILE = 256
+
+
+def partner_of(me, k, owners):
+    result = 0
+    bit = 1
+    while bit < owners:
+        digit = (me // bit) % 2
+        result = result + bit * ((1 - digit) if k & bit else digit)
+        bit *= 2
+    return result
+
+
+def exchange_kernel(
+    owners,
+    send_tokens,
+    send_grads,
+    w_gate,
+    w_up,
+    w_down,
+    got_tokens,
+    got_grads,
+    hidden,
+    grad_gate,
+    grad_up,
+    returned,
+    gate_mat,
+    up_mat,
+    down_mat,
+    part_pre,
+    part_act,
+    peer_pre,
+    peer_act,
+    slot_grad,
+    load_sem,
+    own_sem,
+    tok_send,
+    tok_recv,
+    grad_send,
+    grad_recv,
+    pre_send,
+    pre_recv,
+    act_send,
+    act_recv,
+    back_send,
+    back_recv,
+):
+    me = lax.axis_index("expert")
+    other = 1 - lax.axis_index("dp")
+    depth, width = w_gate.shape
+    mesh_ids = pl.DeviceIdType.MESH
+
+    loads = [
+        pltpu.make_async_copy(source, target, load_sem.at[i])
+        for i, (source, target) in enumerate(
+            ((w_gate, gate_mat), (w_up, up_mat), (w_down, down_mat))
+        )
+    ]
+    for load in loads:
+        load.start()
+    own = [
+        pltpu.make_async_copy(source.at[pl.ds(0, MOST)], target.at[pl.ds(0, MOST)], own_sem.at[i])
+        for i, (source, target) in enumerate(((send_tokens, got_tokens), (send_grads, got_grads)))
+    ]
+    for copy in own:
+        copy.start()
+
+    barrier = pltpu.get_barrier_semaphore()
+    for k in range(1, owners):
+        pl.semaphore_signal(
+            barrier, inc=1, device_id={"expert": partner_of(me, k, owners)}, device_id_type=mesh_ids
+        )
+    pl.semaphore_signal(barrier, inc=1, device_id={"dp": other}, device_id_type=mesh_ids)
+    pl.semaphore_wait(barrier, owners)
+
+    def to_partner(k, source, target, send_sem, recv_sem):
+        rows = pl.ds(k * MOST, MOST)
+        return pltpu.make_async_remote_copy(
+            src_ref=source.at[rows],
+            dst_ref=target.at[rows],
+            send_sem=send_sem.at[k],
+            recv_sem=recv_sem.at[k],
+            device_id={"expert": partner_of(me, k, owners)},
+            device_id_type=mesh_ids,
+        )
+
+    def to_other(g, source, target, send_sem, recv_sem):
+        rows = pl.ds(g * GROUP * MOST, GROUP * MOST)
+        return pltpu.make_async_remote_copy(
+            src_ref=source.at[rows],
+            dst_ref=target.at[rows],
+            send_sem=send_sem.at[g],
+            recv_sem=recv_sem.at[g],
+            device_id={"dp": other},
+            device_id_type=mesh_ids,
+        )
+
+    groups = owners // GROUP
+    tok_copies = {
+        k: to_partner(k, send_tokens, got_tokens, tok_send, tok_recv) for k in range(1, owners)
+    }
+    grad_copies = {
+        k: to_partner(k, send_grads, got_grads, grad_send, grad_recv) for k in range(1, owners)
+    }
+    pre_copies = [to_other(g, part_pre, peer_pre, pre_send, pre_recv) for g in range(groups)]
+    act_copies = [to_other(g, part_act, peer_act, act_send, act_recv) for g in range(groups)]
+    back_copies = {
+        k: to_partner(k, slot_grad, returned, back_send, back_recv) for k in range(1, owners)
+    }
+
+    half = owners // 2
+    near = list(range(1, half))
+    far = list(range(half, owners))
+    for copies in (tok_copies, grad_copies):
+        for i in range(GROUP):
+            copies[far[i]].start()
+            for k in near[2 * i : 2 * i + 2]:
+                copies[k].start()
+    for first in range(GROUP, half, GROUP):
+        for copies in (tok_copies, grad_copies):
+            for k in far[first : first + GROUP]:
+                copies[k].start()
+
+    def members(g):
+        return range(g * GROUP, (g + 1) * GROUP)
+
+    def arrive(g, copies, own_copy):
+        for k in members(g):
+            if k == 0:
+                own_copy.wait()
+            else:
+                copies[k].wait_recv()
+
+    def pre_stage(g):
+        arrive(g, tok_copies, own[0])
+        rows = pl.ds(g * GROUP * MOST, GROUP * MOST)
+
+        @pl.loop(0, width // TILE)
+        def _(c):
+            cols = pl.ds(pl.multiple_of(c * TILE, TILE), TILE)
+            up_cols = pl.ds(pl.multiple_of(width + c * TILE, TILE), TILE)
+            block = got_tokens[rows, :]
+            part_pre[rows, cols] = jnp.dot(
+                block, gate_mat[:, cols], preferred_element_type=jnp.float32
+            ).astype(jnp.bfloat16)
+            part_pre[rows, up_cols] = jnp.dot(
+                block, up_mat[:, cols], preferred_element_type=jnp.float32
+            ).astype(jnp.bfloat16)
+
+        pre_copies[g].start()
+
+    def act_stage(g):
+        arrive(g, grad_copies, own[1])
+        rows = pl.ds(g * GROUP * MOST, GROUP * MOST)
+
+        @pl.loop(0, width // TILE)
+        def _(c):
+            cols = pl.ds(pl.multiple_of(c * TILE, TILE), TILE)
+            part_act[rows, cols] = lax.dot_general(
+                got_grads[rows, :],
+                down_mat[cols, :],
+                contract_cols,
+                preferred_element_type=jnp.float32,
+            ).astype(jnp.bfloat16)
+
+        act_copies[g].start()
+
+    def back_stage(g):
+        pre_copies[g].wait_recv()
+        act_copies[g].wait_recv()
+        rows = pl.ds(g * GROUP * MOST, GROUP * MOST)
+
+        @pl.loop(0, width // TILE)
+        def _(c):
+            cols = pl.ds(pl.multiple_of(c * TILE, TILE), TILE)
+            up_cols = pl.ds(pl.multiple_of(width + c * TILE, TILE), TILE)
+
+            def total(part, peer, where):
+                return part[rows, where].astype(jnp.float32) + peer[rows, where].astype(jnp.float32)
+
+            parts = local_grads(
+                total(part_pre, peer_pre, cols),
+                total(part_pre, peer_pre, up_cols),
+                total(part_act, peer_act, cols),
+            )
+            hidden[rows, cols], grad_gate[rows, cols], grad_up[rows, cols] = parts
+
+        @pl.loop(0, depth // TILE)
+        def _(c):
+            cols = pl.ds(pl.multiple_of(c * TILE, TILE), TILE)
+            sums = lax.dot_general(
+                grad_gate[rows, :],
+                gate_mat[cols, :],
+                contract_cols,
+                preferred_element_type=jnp.float32,
+            ) + lax.dot_general(
+                grad_up[rows, :],
+                up_mat[cols, :],
+                contract_cols,
+                preferred_element_type=jnp.float32,
+            )
+            slot_grad[rows, cols] = sums.astype(jnp.bfloat16)
+
+        for k in members(g):
+            if k == 0:
+                returned[pl.ds(0, MOST), :] = slot_grad[pl.ds(0, MOST), :]
+            else:
+                back_copies[k].start()
+
+    for load in loads:
+        load.wait()
+    near_groups = groups // 2
+    for g in range(near_groups):
+        pre_stage(g)
+    for g in range(near_groups, groups):
+        if g == near_groups:
+            pre_stage(g)
+            for early in range(near_groups):
+                act_stage(early)
+            act_stage(g)
+            for early in range(near_groups):
+                back_stage(early)
+            back_stage(g)
+        else:
+            pre_stage(g)
+            act_stage(g)
+            back_stage(g)
+
+    for copies in (tok_copies, grad_copies):
+        for copy in copies.values():
+            copy.wait_send()
+    for g in range(groups):
+        pre_copies[g].wait_send()
+        act_copies[g].wait_send()
+    for copy in back_copies.values():
+        copy.wait()
+
+
+def exchange(owners, send_tokens, send_grads, gate_mat, up_mat, down_mat):
+    slots, depth = send_tokens.shape
+    width = gate_mat.shape[1]
+    groups = owners // GROUP
+    bf16 = jnp.bfloat16
+    wide = jax.ShapeDtypeStruct((slots, depth), bf16)
+    thin = jax.ShapeDtypeStruct((slots, width), bf16)
+    dma = pltpu.SemaphoreType.DMA
+    return pl.pallas_call(
+        functools.partial(exchange_kernel, owners),
+        out_shape=(wide, wide, thin, thin, thin, wide),
+        in_specs=[pl.BlockSpec(memory_space=pl.ANY)] * 5,
+        out_specs=[pl.BlockSpec(memory_space=pltpu.VMEM)] * 6,
+        scratch_shapes=[
+            pltpu.VMEM((depth, width), bf16),
+            pltpu.VMEM((depth, width), bf16),
+            pltpu.VMEM((width, depth), bf16),
+            pltpu.VMEM((slots, 2 * width), bf16),
+            pltpu.VMEM((slots, width), bf16),
+            pltpu.VMEM((slots, 2 * width), bf16),
+            pltpu.VMEM((slots, width), bf16),
+            pltpu.VMEM((slots, depth), bf16),
+            dma((3,)),
+            dma((2,)),
+        ]
+        + [dma((owners,))] * 4
+        + [dma((groups,))] * 4
+        + [dma((owners,))] * 2,
+        compiler_params=pltpu.CompilerParams(
+            collective_id=0, has_side_effects=True, vmem_limit_bytes=56 * 1024 * 1024
+        ),
+        cost_estimate=pl.CostEstimate(
+            flops=10 * slots * depth * width,
+            bytes_accessed=6 * depth * width + 10 * slots * depth + 6 * slots * width,
+            transcendentals=slots * width,
+        ),
+        name="exchange",
+    )(send_tokens, send_grads, gate_mat, up_mat, down_mat)
+
+
+def fused_shards(tokens, out_grad, expert_ids, gate_probs, w_gate, w_up, w_down):
+    tok_rows = tokens.shape[0]
+    owners = lax.axis_size("expert")
+    slots = owners * MOST
+    me = lax.axis_index("expert").astype(jnp.int32)
+    pick_ids = expert_ids.T.reshape(-1)
+    onehot = (pick_ids[:, None] == jnp.arange(owners, dtype=jnp.int32)[None, :]).astype(jnp.int32)
+    rank_in = jnp.sum((jnp.cumsum(onehot, axis=0) - 1) * onehot, axis=1)
+    slot_of = ((pick_ids ^ me) * MOST + rank_in).reshape(2, tok_rows)
+    slot_ids = jnp.arange(slots, dtype=jnp.int32)[:, None]
+    first = slot_ids == slot_of[0][None, :]
+    second = slot_ids == slot_of[1][None, :]
+    placing = (first | second).astype(jnp.bfloat16)
+    slot_prob = jnp.sum(
+        jnp.where(first, gate_probs[:, 0][None, :], 0.0)
+        + jnp.where(second, gate_probs[:, 1][None, :], 0.0),
+        axis=1,
+    )
+    send_tokens = jnp.dot(placing, tokens, preferred_element_type=jnp.float32).astype(jnp.bfloat16)
+    send_grads = (
+        slot_prob[:, None] * jnp.dot(placing, out_grad, preferred_element_type=jnp.float32)
+    ).astype(jnp.bfloat16)
+    got_tokens, got_grads, hidden, grad_gate, grad_up, returned = exchange(
+        owners, send_tokens, send_grads, w_gate[0], w_up[0], w_down[0]
+    )
+
+    def outer(left, right):
+        return lax.dot_general(left, right, contract_rows, preferred_element_type=jnp.float32)[None]
+
+    token_grad = lax.dot_general(
+        placing, returned, contract_rows, preferred_element_type=jnp.float32
+    ).astype(jnp.bfloat16)
+    return (
+        token_grad,
+        outer(got_tokens, grad_gate),
+        outer(got_tokens, grad_up),
+        outer(hidden, got_grads),
+    )
+
+
+def fits_fused(mesh):
+    owners = mesh.shape["expert"]
+    return mesh.shape["dp"] == 2 and owners == 4 * GROUP
+
+
 def solution(mesh):
     in_specs = (
         P("expert", "dp"),
@@ -113,4 +441,5 @@
         P("expert", "dp", None),
         P("expert", None, "dp"),
     )
-    return jax.shard_map(shards, mesh=mesh, in_specs=in_specs, out_specs=out_specs, check_vma=False)
+    body = fused_shards if fits_fused(mesh) else shards
+    return jax.shard_map(body, mesh=mesh, in_specs=in_specs, out_specs=out_specs, check_vma=False)

time: 298 us -> 185 us (0.62)
  the two profiles are of different devices: /device:TPU:0 before, /device:TPU:9 now
where the time goes in v1:
time: 185 us
  Pallas kernels  155 us (84%)
  matrix products  24.9 us (13%)
  local copies, waits for them, and re-layouts  2.54 us (1%)
    pallas_call x1, Pallas kernels, exchange(): pl.pallas_call(functools.partial(exchange_kernel, owners), out_shape=(wid...  155 us
    dot_general x3, matrix products, outer(): lax.dot_general(left, right, contract_rows, preferred_element_type=jnp.fl...  17.4 us

profile of v1, /device:TPU:9, one launch (start us, length us, event | category | flops | bytes accessed | tf_op | source)
XLA Modules:
  0.0 184.5 jit_solution(6741673409041192292)
XLA Ops:
  0.6 0.0 copy-start
  0.6 0.0 copy-start.1
  0.7 0.8 eq.53
  1.5 0.7 copy.14
  2.2 0.8 fusion.13
  3.0 1.2 reduce-window.6
  4.1 0.2 slice_reduce_fusion
  4.4 0.1 fusion.11
  4.5 0.2 add_reduce_fusion
  4.7 0.0 copy-done
  4.7 2.0 %multiply_convert_fusion.send_grads = bf16[512,2048]{1,0:T(8,128)(2,1)} fusion(bf16[256,2048]{1,0:T(8,128)(2,1)S(1)} %copy-done, f32[512]{0:T(512)S(1)} %add_reduce_fusion, s32[256]{0:T(256)S(1)} %get-tuple-element.19, s32[256]{0:T(256)S(1)} %get-tuple-element.18), kind=kOutput, calls=%fused_computation.3 | convolution fusion | flops 539361280 | bytes 3149824 | tf_op jit(solution)/shard_map/dot_general | solution.py:403
  6.7 0.0 copy-done.1
  6.7 2.0 %convolution_convert_fusion.send_tokens = bf16[512,2048]{1,0:T(8,128)(2,1)} fusion(bf16[256,2048]{1,0:T(8,128)(2,1)S(1)} %copy-done.1, s32[256]{0:T(256)S(1)} %get-tuple-element.19, s32[256]{0:T(256)S(1)} %get-tuple-element.18), kind=kOutput, calls=%fused_computation.4 | convolution fusion | flops 538312704 | bytes 3147776 | tf_op jit(solution)/shard_map/dot_general | solution.py:401
  8.8 154.8 %exchange.1 = (bf16[512,2048]{1,0:T(8,128)(2,1)}, bf16[512,2048]{1,0:T(8,128)(2,1)}, bf16[512,1024]{1,0:T(8,128)(2,1)}, bf16[512,1024]{1,0:T(8,128)(2,1)}, bf16[...) custom-call(bf16[512,2048]{1,0:T(8,128)(2,1)} %convolution_convert_fusion.send_tokens, ...), custom_call_target="tpu_custom_call" | custom-call | flops 10737418240 | bytes 26214400 | tf_op jit(solution)/shard_map/exchange/pallas_call | solution.py:351
  163.6 0.0 copy-start.2
  163.6 0.0 copy-start.4
  163.6 3.5 %convolution_convert_fusion.1 = bf16[256,2048]{1,0:T(8,128)(2,1)} fusion(bf16[512,2048]{1,0:T(8,128)(2,1)} %get-tuple-element.10, s32[256]{0:T(256)S(1)} %get-tuple-element.19, s32[256]{0:T(256)S(1)} %get-tuple-element.18), kind=kOutput, calls=%fused_computation.5 | convolution fusion | flops 537788416 | bytes 3147776 | tf_op jit(solution)/shard_map/dot_general | solution.py:412
  167.1 0.0 copy-done.2
  167.1 0.0 copy-done.4
  167.1 5.8 %convolution_bitcast_fusion.2 = f32[1,2048,1024]{2,1,0:T(8,128)} fusion(bf16[512,2048]{1,0:T(8,128)(2,1)S(1)} %copy-done.2, bf16[512,1024]{1,0:T(8,128)(2,1)S(1)} %copy-done.4), kind=kOutput, calls=%fused_computation.2 | convolution fusion | flops 2147483648 | bytes 11534336 | tf_op jit(solution)/shard_map/dot_general | solution.py:410
  172.9 0.0 copy-done.3
  172.9 5.8 %convolution_bitcast_fusion.1 = f32[1,2048,1024]{2,1,0:T(8,128)} fusion(bf16[512,2048]{1,0:T(8,128)(2,1)S(1)} %copy-done.2, bf16[512,1024]{1,0:T(8,128)(2,1)S(1)} %copy-done.3), kind=kOutput, calls=%fused_computation.1 | convolution fusion | flops 2147483648 | bytes 11534336 | tf_op jit(solution)/shard_map/dot_general | solution.py:410
  178.7 0.0 copy-done.6
  178.7 5.8 %convolution_bitcast_fusion = f32[1,1024,2048]{2,1,0:T(8,128)} fusion(bf16[512,1024]{1,0:T(8,128)(2,1)S(1)} %copy-done.6, bf16[512,2048]{1,0:T(8,128)(2,1)S(1)} %copy-done.5), kind=kOutput, calls=%fused_computation | convolution fusion | flops 2147483648 | bytes 11534336 | tf_op jit(solution)/shard_map/dot_general | solution.py:410
  (9 shorter events, 0.1 us)
Async XLA Ops:
  0.6 4.1 %copy-start = (bf16[256,2048]{1,0:T(8,128)(2,1)S(1)}, bf16[256,2048]{1,0:T(8,128)(2,1)}, u32[]{:S(2)}) copy-start(bf16[256,2048]{1,0:T(8,128)(2,1)} %param.8) | copy-start | bytes 3145732
  0.6 6.1 %copy-start.1 = (bf16[256,2048]{1,0:T(8,128)(2,1)S(1)}, bf16[256,2048]{1,0:T(8,128)(2,1)}, u32[]{:S(2)}) copy-start(bf16[256,2048]{1,0:T(8,128)(2,1)} %param.7) | copy-start | bytes 3145732
  163.6 3.5 %copy-start.2 = (bf16[512,2048]{1,0:T(8,128)(2,1)S(1)}, bf16[512,2048]{1,0:T(8,128)(2,1)}, u32[]{:S(2)}) copy-start(bf16[512,2048]{1,0:T(8,128)(2,1)} %get-tuple-element.11) | copy-start | bytes 6291460
  163.6 3.5 %copy-start.4 = (bf16[512,1024]{1,0:T(8,128)(2,1)S(1)}, bf16[512,1024]{1,0:T(8,128)(2,1)}, u32[]{:S(2)}) copy-start(bf16[512,1024]{1,0:T(8,128)(2,1)} %get-tuple-element.12) | copy-start | bytes 3145732
  167.1 5.8 %copy-start.3 = (bf16[512,1024]{1,0:T(8,128)(2,1)S(1)}, bf16[512,1024]{1,0:T(8,128)(2,1)}, u32[]{:S(2)}) copy-start(bf16[512,1024]{1,0:T(8,128)(2,1)} %get-tuple-element.13) | copy-start | bytes 3145732
  172.9 5.8 %copy-start.5 = (bf16[512,2048]{1,0:T(8,128)(2,1)S(1)}, bf16[512,2048]{1,0:T(8,128)(2,1)}, u32[]{:S(2)}) copy-start(bf16[512,2048]{1,0:T(8,128)(2,1)} %get-tuple-element.15) | copy-start | bytes 6291460
  172.9 5.8 %copy-start.6 = (bf16[512,1024]{1,0:T(8,128)(2,1)S(1)}, bf16[512,1024]{1,0:T(8,128)(2,1)}, u32[]{:S(2)}) copy-start(bf16[512,1024]{1,0:T(8,128)(2,1)} %get-tuple-element.14) | copy-start | bytes 3145732

commit v2 on v1

--- a/solution.py
+++ b/solution.py
@@ -128,6 +128,10 @@
     grad_gate,
     grad_up,
     returned,
+    last_a,
+    last_b,
+    last_c,
+    last_d,
     gate_mat,
     up_mat,
     down_mat,
@@ -209,8 +213,10 @@
     pre_copies = [to_other(g, part_pre, peer_pre, pre_send, pre_recv) for g in range(groups)]
     act_copies = [to_other(g, part_act, peer_act, act_send, act_recv) for g in range(groups)]
     back_copies = {
-        k: to_partner(k, slot_grad, returned, back_send, back_recv) for k in range(1, owners)
+        k: to_partner(k, slot_grad, returned, back_send, back_recv)
+        for k in range(1, owners - GROUP)
     }
+    last = (last_a, last_b, last_c, last_d)
 
     half = owners // 2
     near = list(range(1, half))
@@ -254,7 +260,6 @@
         pre_copies[g].start()
 
     def act_stage(g):
-        arrive(g, grad_copies, own[1])
         rows = pl.ds(g * GROUP * MOST, GROUP * MOST)
 
         @pl.loop(0, width // TILE)
@@ -303,8 +308,14 @@
                 contract_cols,
                 preferred_element_type=jnp.float32,
             )
-            slot_grad[rows, cols] = sums.astype(jnp.bfloat16)
-
+            sums = sums.astype(jnp.bfloat16)
+            if g < groups - 1:
+                slot_grad[rows, cols] = sums
+            else:
+                for i in range(GROUP):
+                    last[i][:, cols] = sums[i * MOST : (i + 1) * MOST]
+
+    def send_back(g):
         for k in members(g):
             if k == 0:
                 returned[pl.ds(0, MOST), :] = slot_grad[pl.ds(0, MOST), :]
@@ -314,21 +325,20 @@
     for load in loads:
         load.wait()
     near_groups = groups // 2
+    for g in range(near_groups + 1):
+        pre_stage(g)
+    for g in range(near_groups + 1):
+        arrive(g, grad_copies, own[1])
+        act_stage(g)
     for g in range(near_groups):
-        pre_stage(g)
-    for g in range(near_groups, groups):
-        if g == near_groups:
-            pre_stage(g)
-            for early in range(near_groups):
-                act_stage(early)
-            act_stage(g)
-            for early in range(near_groups):
-                back_stage(early)
-            back_stage(g)
-        else:
-            pre_stage(g)
-            act_stage(g)
-            back_stage(g)
+        back_stage(g)
+        send_back(g)
+    back_stage(near_groups)
+    pre_stage(groups - 1)
+    arrive(groups - 1, grad_copies, own[1])
+    send_back(near_groups)
+    act_stage(groups - 1)
+    back_stage(groups - 1)
 
     for copies in (tok_copies, grad_copies):
         for copy in copies.values():
@@ -346,13 +356,15 @@
     groups = owners // GROUP
     bf16 = jnp.bfloat16
     wide = jax.ShapeDtypeStruct((slots, depth), bf16)
+    back = jax.ShapeDtypeStruct((slots - GROUP * MOST, depth), bf16)
+    piece = jax.ShapeDtypeStruct((MOST, depth), bf16)
     thin = jax.ShapeDtypeStruct((slots, width), bf16)
     dma = pltpu.SemaphoreType.DMA
     return pl.pallas_call(
         functools.partial(exchange_kernel, owners),
-        out_shape=(wide, wide, thin, thin, thin, wide),
+        out_shape=(wide, wide, thin, thin, thin, back) + (piece,) * GROUP,
         in_specs=[pl.BlockSpec(memory_space=pl.ANY)] * 5,
-        out_specs=[pl.BlockSpec(memory_space=pltpu.VMEM)] * 6,
+        out_specs=[pl.BlockSpec(memory_space=pltpu.VMEM)] * (6 + GROUP),
         scratch_shapes=[
             pltpu.VMEM((depth, width), bf16),
             pltpu.VMEM((depth, width), bf16),
@@ -361,13 +373,13 @@
             pltpu.VMEM((slots, width), bf16),
             pltpu.VMEM((slots, 2 * width), bf16),
             pltpu.VMEM((slots, width), bf16),
-            pltpu.VMEM((slots, depth), bf16),
+            pltpu.VMEM((slots - GROUP * MOST, depth), bf16),
             dma((3,)),
             dma((2,)),
         ]
         + [dma((owners,))] * 4
         + [dma((groups,))] * 4
-        + [dma((owners,))] * 2,
+        + [dma((owners - GROUP,))] * 2,
         compiler_params=pltpu.CompilerParams(
             collective_id=0, has_side_effects=True, vmem_limit_bytes=56 * 1024 * 1024
         ),
@@ -402,16 +414,29 @@
     send_grads = (
         slot_prob[:, None] * jnp.dot(placing, out_grad, preferred_element_type=jnp.float32)
     ).astype(jnp.bfloat16)
-    got_tokens, got_grads, hidden, grad_gate, grad_up, returned = exchange(
+    got_tokens, got_grads, hidden, grad_gate, grad_up, returned, *last = exchange(
         owners, send_tokens, send_grads, w_gate[0], w_up[0], w_down[0]
     )
+
+    early = slots - GROUP * MOST
+    last = [
+        lax.ppermute(rows, "expert", [(i, i ^ (owners - GROUP + k)) for i in range(owners)])
+        for k, rows in enumerate(last)
+    ]
 
     def outer(left, right):
         return lax.dot_general(left, right, contract_rows, preferred_element_type=jnp.float32)[None]
 
     token_grad = lax.dot_general(
-        placing, returned, contract_rows, preferred_element_type=jnp.float32
-    ).astype(jnp.bfloat16)
+        placing[:early], returned, contract_rows, preferred_element_type=jnp.float32
+    )
+    token_grad = token_grad + lax.dot_general(
+        placing[early:],
+        jnp.concatenate(last, axis=0),
+        contract_rows,
+        preferred_element_type=jnp.float32,
+    )
+    token_grad = token_grad.astype(jnp.bfloat16)
     return (
         token_grad,
         outer(got_tokens, grad_gate),

time: 185 us -> 170 us (0.919)
  the two profiles are of different devices: /device:TPU:9 before, /device:TPU:0 now
where the time goes in v2:
time: 170 us
  Pallas kernels  131 us (77%)
  matrix products  25.7 us (15%)
  starting transfers between devices  8.05 us (5%)
  local copies, waits for them, and re-layouts  2.54 us (1%)
    pallas_call x1, Pallas kernels, exchange(): pl.pallas_call(functools.partial(exchange_kernel, owners), out_shape=(wid...  131 us
    dot_general x3, matrix products, outer(): lax.dot_general(left, right, contract_rows, preferred_element_type=jnp.fl...  19.4 us
    ppermute x4, starting transfers between devices, fused_shards(): lax.ppermute(rows, 'expert', [(i, i ^ owners - GROUP + k) for i in range(...  8.05 us
  transfers between devices with their start and end apart: 4, of which 0 were waited for; matrix products, arithmetic and copies ran while one was open for 12% of the time, Pallas kernels for 0%

profile of v2, /device:TPU:0, one launch (start us, length us, event | category | flops | bytes accessed | tf_op | source)
XLA Modules:
  0.0 169.5 jit_solution(12445055723312535601)
XLA Ops:
  0.6 0.0 copy-start
  0.7 0.8 eq.53
  1.5 0.7 copy.14
  2.2 0.8 fusion.18
  3.0 1.2 reduce-window.6
  4.1 0.2 slice_reduce_fusion
  4.4 0.1 fusion.13
  4.5 2.0 %convolution_convert_fusion.send_tokens = bf16[512,2048]{1,0:T(8,128)(2,1)} fusion(bf16[256,2048]{1,0:T(8,128)(2,1)S(1)} %copy-done, s32[256]{0:T(256)S(1)} %get-tuple-element.27, s32[256]{0:T(256)S(1)} %get-tuple-element.26), kind=kOutput, calls=%fused_computation.4 | convolution fusion | flops 538312704 | bytes 3147776 | tf_op jit(solution)/shard_map/dot_general | solution.py:413
  6.5 0.2 add_reduce_fusion
  6.7 2.0 %multiply_convert_fusion.send_grads = bf16[512,2048]{1,0:T(8,128)(2,1)} fusion(bf16[256,2048]{1,0:T(8,128)(2,1)S(1)} %copy-done.2, f32[512]{0:T(512)S(1)} %add_reduce_fusion, s32[256]{0:T(256)S(1)} %get-tuple-element.27, s32[256]{0:T(256)S(1)} %get-tuple-element.26), kind=kOutput, calls=%fused_computation.3 | convolution fusion | flops 539361280 | bytes 3149824 | tf_op jit(solution)/shard_map/dot_general | solution.py:415
  8.8 130.9 %exchange.1 = (bf16[512,2048]{1,0:T(8,128)(2,1)}, bf16[512,2048]{1,0:T(8,128)(2,1)}, bf16[512,1024]{1,0:T(8,128)(2,1)}, bf16[512,1024]{1,0:T(8,128)(2,1)}, bf16[...) custom-call(bf16[512,2048]{1,0:T(8,128)(2,1)} %convolution_convert_f, ...), custom_call_target="tpu_custom_call" | custom-call | flops 10737418240 | bytes 26214400 | tf_op jit(solution)/shard_map/exchange/pallas_call | solution.py:363
  139.6 1.5 collective-permute-start
  141.1 1.9 %collective-permute-start.1 = (bf16[32,2048]{1,0:T(8,128)(2,1)}, bf16[32,2048]{1,0:T(8,128)(2,1)S(1)}, u32[]{:S(2)}, u32[]{:S(2)}) collective-permute-start(bf16[32,2048]{1,0:T(8,128)(2,1)} %get-tuple-element.16), channel_id=1, source_target_pairs={{0,13},{1,12},{2,15},{3,14},{4,9},{5,8},{6,11},{7,10},{8,5},{9,4},... | collective-permute-start | bytes 393224 | tf_op jit(solution)/shard_map/ppermute | solution.py:423
  143.0 1.1 collective-permute-start.2
  144.1 3.6 %collective-permute-start.3 = (bf16[32,2048]{1,0:T(8,128)(2,1)}, bf16[32,2048]{1,0:T(8,128)(2,1)S(1)}, u32[]{:S(2)}, u32[]{:S(2)}) collective-permute-start(bf16[32,2048]{1,0:T(8,128)(2,1)} %get-tuple-element.18), channel_id=1, source_target_pairs={{0,15},{1,14},{2,13},{3,12},{4,11},{5,10},{6,9},{7,8},{8,7},{9,6},... | collective-permute-start | bytes 393224 | tf_op jit(solution)/shard_map/ppermute | solution.py:423
  147.7 0.1 fusion.8
  147.8 7.8 %convolution_bitcast_fusion.2 = f32[1,2048,1024]{2,1,0:T(8,128)} fusion(bf16[512,2048]{1,0:T(8,128)(2,1)} %get-tuple-element.19, bf16[512,1024]{1,0:T(8,128)(2,1)} %get-tuple-element.20), kind=kOutput, calls=%fused_computation.2 | convolution fusion | flops 2147483648 | bytes 11534336 | tf_op jit(solution)/shard_map/dot_general | solution.py:428
  155.6 5.8 %convolution_bitcast_fusion.1 = f32[1,2048,1024]{2,1,0:T(8,128)} fusion(bf16[512,2048]{1,0:T(8,128)(2,1)S(1)} %copy-done.3, bf16[512,1024]{1,0:T(8,128)(2,1)S(1)} %copy-done.4), kind=kOutput, calls=%fused_computation.1 | convolution fusion | flops 2147483648 | bytes 11534336 | tf_op jit(solution)/shard_map/dot_general | solution.py:428
  161.4 5.8 %convolution_bitcast_fusion = f32[1,1024,2048]{2,1,0:T(8,128)} fusion(bf16[512,1024]{1,0:T(8,128)(2,1)S(1)} %copy-done.6, bf16[512,2048]{1,0:T(8,128)(2,1)S(1)} %copy-done.5), kind=kOutput, calls=%fused_computation | convolution fusion | flops 2147483648 | bytes 11534336 | tf_op jit(solution)/shard_map/dot_general | solution.py:428
  167.2 0.8 fusion.9
  168.0 0.0 collective-permute-done
  168.0 0.0 collective-permute-done.1
  168.0 0.0 collective-permute-done.2
  168.1 1.5 fusion
  (19 shorter events, 0.1 us)
Async XLA Ops:
  0.6 3.9 %copy-start = (bf16[256,2048]{1,0:T(8,128)(2,1)S(1)}, bf16[256,2048]{1,0:T(8,128)(2,1)}, u32[]{:S(2)}) copy-start(bf16[256,2048]{1,0:T(8,128)(2,1)} %param.7) | copy-start | bytes 3145732
  0.6 6.1 %copy-start.2 = (bf16[256,2048]{1,0:T(8,128)(2,1)S(1)}, bf16[256,2048]{1,0:T(8,128)(2,1)}, u32[]{:S(2)}) copy-start(bf16[256,2048]{1,0:T(8,128)(2,1)} %param.8) | copy-start | bytes 3145732
  139.6 28.4 %collective-permute-start = (bf16[32,2048]{1,0:T(8,128)(2,1)}, bf16[32,2048]{1,0:T(8,128)(2,1)S(1)}, u32[]{:S(2)}, u32[]{:S(2)}) collective-permute-start(bf16[32,2048]{1,0:T(8,128)(2,1)} %get-tuple-element.15), channel_id=1, source_target_pairs={{0,12},{1,13},{2,14},{3,15},{4,8},{5,9},{6,10},{7,11},{8,4},{9,5},... | collective-permute-start | bytes 393224 | tf_op jit(solution)/shard_map/ppermute | solution.py:423
  141.1 26.9 %collective-permute-start.1 = (bf16[32,2048]{1,0:T(8,128)(2,1)}, bf16[32,2048]{1,0:T(8,128)(2,1)S(1)}, u32[]{:S(2)}, u32[]{:S(2)}) collective-permute-start(bf16[32,2048]{1,0:T(8,128)(2,1)} %get-tuple-element.16), channel_id=1, source_target_pairs={{0,13},{1,12},{2,15},{3,14},{4,9},{5,8},{6,11},{7,10},{8,5},{9,4},... | collective-permute-start | bytes 393224 | tf_op jit(solution)/shard_map/ppermute | solution.py:423
  143.0 25.1 %collective-permute-start.2 = (bf16[32,2048]{1,0:T(8,128)(2,1)}, bf16[32,2048]{1,0:T(8,128)(2,1)S(1)}, u32[]{:S(2)}, u32[]{:S(2)}) collective-permute-start(bf16[32,2048]{1,0:T(8,128)(2,1)} %get-tuple-element.17), channel_id=1, source_target_pairs={{0,14},{1,15},{2,12},{3,13},{4,10},{5,11},{6,8},{7,9},{8,6},{9,7},... | collective-permute-start | bytes 393224 | tf_op jit(solution)/shard_map/ppermute | solution.py:423
  144.1 23.9 %collective-permute-start.3 = (bf16[32,2048]{1,0:T(8,128)(2,1)}, bf16[32,2048]{1,0:T(8,128)(2,1)S(1)}, u32[]{:S(2)}, u32[]{:S(2)}) collective-permute-start(bf16[32,2048]{1,0:T(8,128)(2,1)} %get-tuple-element.18), channel_id=1, source_target_pairs={{0,15},{1,14},{2,13},{3,12},{4,11},{5,10},{6,9},{7,8},{8,7},{9,6},... | collective-permute-start | bytes 393224 | tf_op jit(solution)/shard_map/ppermute | solution.py:423
  147.8 7.8 %copy-start.3 = (bf16[512,2048]{1,0:T(8,128)(2,1)S(1)}, bf16[512,2048]{1,0:T(8,128)(2,1)}, u32[]{:S(2)}) copy-start(bf16[512,2048]{1,0:T(8,128)(2,1)} %get-tuple-element.19) | copy-start | bytes 6291460
  147.8 7.8 %copy-start.4 = (bf16[512,1024]{1,0:T(8,128)(2,1)S(1)}, bf16[512,1024]{1,0:T(8,128)(2,1)}, u32[]{:S(2)}) copy-start(bf16[512,1024]{1,0:T(8,128)(2,1)} %get-tuple-element.21) | copy-start | bytes 3145732
  155.6 5.8 %copy-start.5 = (bf16[512,2048]{1,0:T(8,128)(2,1)S(1)}, bf16[512,2048]{1,0:T(8,128)(2,1)}, u32[]{:S(2)}) copy-start(bf16[512,2048]{1,0:T(8,128)(2,1)} %get-tuple-element.23) | copy-start | bytes 6291460
  155.6 5.8 %copy-start.6 = (bf16[512,1024]{1,0:T(8,128)(2,1)S(1)}, bf16[512,1024]{1,0:T(8,128)(2,1)}, u32[]{:S(2)}) copy-start(bf16[512,1024]{1,0:T(8,128)(2,1)} %get-tuple-element.22) | copy-start | bytes 3145732
  161.4 5.8 %copy-start.1 = (bf16[384,2048]{1,0:T(8,128)(2,1)S(1)}, bf16[384,2048]{1,0:T(8,128)(2,1)}, u32[]{:S(2)}) copy-start(bf16[384,2048]{1,0:T(8,128)(2,1)} %get-tuple-element.14) | copy-start | bytes 4718596

commit v3 on v2

--- a/solution.py
+++ b/solution.py
@@ -315,8 +315,8 @@
                 for i in range(GROUP):
                     last[i][:, cols] = sums[i * MOST : (i + 1) * MOST]
 
-    def send_back(g):
-        for k in members(g):
+    def send_back(rows):
+        for k in rows:
             if k == 0:
                 returned[pl.ds(0, MOST), :] = slot_grad[pl.ds(0, MOST), :]
             else:
@@ -332,11 +332,13 @@
         act_stage(g)
     for g in range(near_groups):
         back_stage(g)
-        send_back(g)
+        send_back(members(g))
     back_stage(near_groups)
+    held = members(near_groups)[GROUP // 2 :]
+    send_back(members(near_groups)[: GROUP // 2])
     pre_stage(groups - 1)
     arrive(groups - 1, grad_copies, own[1])
-    send_back(near_groups)
+    send_back(held)
     act_stage(groups - 1)
     back_stage(groups - 1)
 
@@ -398,8 +400,9 @@
     slots = owners * MOST
     me = lax.axis_index("expert").astype(jnp.int32)
     pick_ids = expert_ids.T.reshape(-1)
-    onehot = (pick_ids[:, None] == jnp.arange(owners, dtype=jnp.int32)[None, :]).astype(jnp.int32)
-    rank_in = jnp.sum((jnp.cumsum(onehot, axis=0) - 1) * onehot, axis=1)
+    order = jnp.arange(2 * tok_rows, dtype=jnp.int32)
+    earlier = (pick_ids[:, None] == pick_ids[None, :]) & (order[:, None] < order[None, :])
+    rank_in = jnp.sum(earlier.astype(jnp.int32), axis=0)
     slot_of = ((pick_ids ^ me) * MOST + rank_in).reshape(2, tok_rows)
     slot_ids = jnp.arange(slots, dtype=jnp.int32)[:, None]
     first = slot_ids == slot_of[0][None, :]

time: 170 us -> 164 us (0.965)
  Pallas kernels: 131 us -> 127 us
    pallas_call x1, Pallas kernels: 131 us -> 127 us  [exchange(): pl.pallas_call(functools.partial(exchange_kernel, owners), out_shape=(wid...]
where the time goes in v3:
time: 164 us
  Pallas kernels  127 us (77%)
  matrix products  25.7 us (16%)
  starting transfers between devices  8.05 us (5%)
    pallas_call x1, Pallas kernels, exchange(): pl.pallas_call(functools.partial(exchange_kernel, owners), out_shape=(wid...  127 us
    dot_general x3, matrix products, outer(): lax.dot_general(left, right, contract_rows, preferred_element_type=jnp.fl...  19.4 us
    ppermute x4, starting transfers between devices, fused_shards(): lax.ppermute(rows, 'expert', [(i, i ^ owners - GROUP + k) for i in range(...  8.05 us
  transfers between devices with their start and end apart: 4, of which 0 were waited for; matrix products, arithmetic and copies ran while one was open for 12% of the time, Pallas kernels for 0%

profile of v3, /device:TPU:0, one launch (start us, length us, event | category | flops | bytes accessed | tf_op | source)
XLA Modules:
  0.0 163.9 jit_solution(7591456176781427726)
XLA Ops:
  0.6 0.0 copy-start
  0.6 0.0 copy-start.2
  0.7 0.8 copy.11
  1.5 0.2 convert_reduce_fusion
  1.7 0.8 fusion.16
  2.4 2.0 %convolution_convert_fusion.send_tokens = bf16[512,2048]{1,0:T(8,128)(2,1)} fusion(bf16[256,2048]{1,0:T(8,128)(2,1)S(1)} %copy-done, s32[256]{0:T(256)S(1)} %get-tuple-element.27, s32[256]{0:T(256)S(1)} %get-tuple-element.26), kind=kOutput, calls=%fused_computation.4 | convolution fusion | flops 538312704 | bytes 3147776 | tf_op jit(solution)/shard_map/dot_general | solution.py:416
  4.5 0.2 add_reduce_fusion
  4.7 2.0 %multiply_convert_fusion.send_grads = bf16[512,2048]{1,0:T(8,128)(2,1)} fusion(bf16[256,2048]{1,0:T(8,128)(2,1)S(1)} %copy-done.2, f32[512]{0:T(512)S(1)} %add_reduce_fusion, s32[256]{0:T(256)S(1)} %get-tuple-element.27, s32[256]{0:T(256)S(1)} %get-tuple-element.26), kind=kOutput, calls=%fused_computation.3 | convolution fusion | flops 539361280 | bytes 3149824 | tf_op jit(solution)/shard_map/dot_general | solution.py:418
  6.7 127.3 %exchange.1 = (bf16[512,2048]{1,0:T(8,128)(2,1)}, bf16[512,2048]{1,0:T(8,128)(2,1)}, bf16[512,1024]{1,0:T(8,128)(2,1)}, bf16[512,1024]{1,0:T(8,128)(2,1)}, bf16[...) custom-call(bf16[512,2048]{1,0:T(8,128)(2,1)} %convolution_convert_f, ...), custom_call_target="tpu_custom_call" | custom-call | flops 10737418240 | bytes 26214400 | tf_op jit(solution)/shard_map/exchange/pallas_call | solution.py:365
  134.0 2.9 %collective-permute-start = (bf16[32,2048]{1,0:T(8,128)(2,1)}, bf16[32,2048]{1,0:T(8,128)(2,1)S(1)}, u32[]{:S(2)}, u32[]{:S(2)}) collective-permute-start(bf16[32,2048]{1,0:T(8,128)(2,1)} %get-tuple-element.15), channel_id=1, source_target_pairs={{0,12},{1,13},{2,14},{3,15},{4,8},{5,9},{6,10},{7,11},{8,4},{9,5},... | collective-permute-start | bytes 393224 | tf_op jit(solution)/shard_map/ppermute | solution.py:426
  136.9 0.6 collective-permute-start.1
  137.5 3.6 %collective-permute-start.2 = (bf16[32,2048]{1,0:T(8,128)(2,1)}, bf16[32,2048]{1,0:T(8,128)(2,1)S(1)}, u32[]{:S(2)}, u32[]{:S(2)}) collective-permute-start(bf16[32,2048]{1,0:T(8,128)(2,1)} %get-tuple-element.17), channel_id=1, source_target_pairs={{0,14},{1,15},{2,12},{3,13},{4,10},{5,11},{6,8},{7,9},{8,6},{9,7},... | collective-permute-start | bytes 393224 | tf_op jit(solution)/shard_map/ppermute | solution.py:426
  141.1 0.9 collective-permute-start.3
  142.1 0.1 fusion.9
  142.2 0.0 copy-start.3
  142.2 7.8 %convolution_bitcast_fusion.2 = f32[1,2048,1024]{2,1,0:T(8,128)} fusion(bf16[512,2048]{1,0:T(8,128)(2,1)} %get-tuple-element.19, bf16[512,1024]{1,0:T(8,128)(2,1)} %get-tuple-element.20), kind=kOutput, calls=%fused_computation.2 | convolution fusion | flops 2147483648 | bytes 11534336 | tf_op jit(solution)/shard_map/dot_general | solution.py:431
  150.0 5.8 %convolution_bitcast_fusion.1 = f32[1,2048,1024]{2,1,0:T(8,128)} fusion(bf16[512,2048]{1,0:T(8,128)(2,1)S(1)} %copy-done.3, bf16[512,1024]{1,0:T(8,128)(2,1)S(1)} %copy-done.4), kind=kOutput, calls=%fused_computation.1 | convolution fusion | flops 2147483648 | bytes 11534336 | tf_op jit(solution)/shard_map/dot_general | solution.py:431
  155.8 5.8 %convolution_bitcast_fusion = f32[1,1024,2048]{2,1,0:T(8,128)} fusion(bf16[512,1024]{1,0:T(8,128)(2,1)S(1)} %copy-done.6, bf16[512,2048]{1,0:T(8,128)(2,1)S(1)} %copy-done.5), kind=kOutput, calls=%fused_computation | convolution fusion | flops 2147483648 | bytes 11534336 | tf_op jit(solution)/shard_map/dot_general | solution.py:431
  161.6 0.8 fusion.10
  162.4 0.0 collective-permute-done
  162.4 0.0 collective-permute-done.1
  162.4 0.0 collective-permute-done.2
  162.4 0.0 collective-permute-done.3
  162.4 1.5 fusion
  (13 shorter events, 0.0 us)
Async XLA Ops:
  0.6 1.8 %copy-start = (bf16[256,2048]{1,0:T(8,128)(2,1)S(1)}, bf16[256,2048]{1,0:T(8,128)(2,1)}, u32[]{:S(2)}) copy-start(bf16[256,2048]{1,0:T(8,128)(2,1)} %param.7) | copy-start | bytes 3145732
  0.6 4.0 %copy-start.2 = (bf16[256,2048]{1,0:T(8,128)(2,1)S(1)}, bf16[256,2048]{1,0:T(8,128)(2,1)}, u32[]{:S(2)}) copy-start(bf16[256,2048]{1,0:T(8,128)(2,1)} %param.8) | copy-start | bytes 3145732
  134.0 28.4 %collective-permute-start = (bf16[32,2048]{1,0:T(8,128)(2,1)}, bf16[32,2048]{1,0:T(8,128)(2,1)S(1)}, u32[]{:S(2)}, u32[]{:S(2)}) collective-permute-start(bf16[32,2048]{1,0:T(8,128)(2,1)} %get-tuple-element.15), channel_id=1, source_target_pairs={{0,12},{1,13},{2,14},{3,15},{4,8},{5,9},{6,10},{7,11},{8,4},{9,5},... | collective-permute-start | bytes 393224 | tf_op jit(solution)/shard_map/ppermute | solution.py:426
  136.9 25.5 %collective-permute-start.1 = (bf16[32,2048]{1,0:T(8,128)(2,1)}, bf16[32,2048]{1,0:T(8,128)(2,1)S(1)}, u32[]{:S(2)}, u32[]{:S(2)}) collective-permute-start(bf16[32,2048]{1,0:T(8,128)(2,1)} %get-tuple-element.16), channel_id=1, source_target_pairs={{0,13},{1,12},{2,15},{3,14},{4,9},{5,8},{6,11},{7,10},{8,5},{9,4},... | collective-permute-start | bytes 393224 | tf_op jit(solution)/shard_map/ppermute | solution.py:426
  137.5 24.9 %collective-permute-start.2 = (bf16[32,2048]{1,0:T(8,128)(2,1)}, bf16[32,2048]{1,0:T(8,128)(2,1)S(1)}, u32[]{:S(2)}, u32[]{:S(2)}) collective-permute-start(bf16[32,2048]{1,0:T(8,128)(2,1)} %get-tuple-element.17), channel_id=1, source_target_pairs={{0,14},{1,15},{2,12},{3,13},{4,10},{5,11},{6,8},{7,9},{8,6},{9,7},... | collective-permute-start | bytes 393224 | tf_op jit(solution)/shard_map/ppermute | solution.py:426
  141.1 21.3 %collective-permute-start.3 = (bf16[32,2048]{1,0:T(8,128)(2,1)}, bf16[32,2048]{1,0:T(8,128)(2,1)S(1)}, u32[]{:S(2)}, u32[]{:S(2)}) collective-permute-start(bf16[32,2048]{1,0:T(8,128)(2,1)} %get-tuple-element.18), channel_id=1, source_target_pairs={{0,15},{1,14},{2,13},{3,12},{4,11},{5,10},{6,9},{7,8},{8,7},{9,6},... | collective-permute-start | bytes 393224 | tf_op jit(solution)/shard_map/ppermute | solution.py:426
  142.2 7.8 %copy-start.3 = (bf16[512,2048]{1,0:T(8,128)(2,1)S(1)}, bf16[512,2048]{1,0:T(8,128)(2,1)}, u32[]{:S(2)}) copy-start(bf16[512,2048]{1,0:T(8,128)(2,1)} %get-tuple-element.19) | copy-start | bytes 6291460
  142.2 7.8 %copy-start.4 = (bf16[512,1024]{1,0:T(8,128)(2,1)S(1)}, bf16[512,1024]{1,0:T(8,128)(2,1)}, u32[]{:S(2)}) copy-start(bf16[512,1024]{1,0:T(8,128)(2,1)} %get-tuple-element.21) | copy-start | bytes 3145732
  150.0 5.8 %copy-start.5 = (bf16[512,2048]{1,0:T(8,128)(2,1)S(1)}, bf16[512,2048]{1,0:T(8,128)(2,1)}, u32[]{:S(2)}) copy-start(bf16[512,2048]{1,0:T(8,128)(2,1)} %get-tuple-element.23) | copy-start | bytes 6291460
  150.0 5.8 %copy-start.6 = (bf16[512,1024]{1,0:T(8,128)(2,1)S(1)}, bf16[512,1024]{1,0:T(8,128)(2,1)}, u32[]{:S(2)}) copy-start(bf16[512,1024]{1,0:T(8,128)(2,1)} %get-tuple-element.22) | copy-start | bytes 3145732
  155.8 5.8 %copy-start.1 = (bf16[384,2048]{1,0:T(8,128)(2,1)S(1)}, bf16[384,2048]{1,0:T(8,128)(2,1)}, u32[]{:S(2)}) copy-start(bf16[384,2048]{1,0:T(8,128)(2,1)} %get-tuple-element.14) | copy-start | bytes 4718596

commit v4 on v3

--- a/solution.py
+++ b/solution.py
@@ -226,10 +226,6 @@
             copies[far[i]].start()
             for k in near[2 * i : 2 * i + 2]:
                 copies[k].start()
-    for first in range(GROUP, half, GROUP):
-        for copies in (tok_copies, grad_copies):
-            for k in far[first : first + GROUP]:
-                copies[k].start()
 
     def members(g):
         return range(g * GROUP, (g + 1) * GROUP)
@@ -327,9 +323,13 @@
     near_groups = groups // 2
     for g in range(near_groups + 1):
         pre_stage(g)
+    for k in far[GROUP:]:
+        tok_copies[k].start()
     for g in range(near_groups + 1):
         arrive(g, grad_copies, own[1])
         act_stage(g)
+    for k in far[GROUP:]:
+        grad_copies[k].start()
     for g in range(near_groups):
         back_stage(g)
         send_back(members(g))
@@ -338,8 +338,8 @@
     send_back(members(near_groups)[: GROUP // 2])
     pre_stage(groups - 1)
     arrive(groups - 1, grad_copies, own[1])
+    act_stage(groups - 1)
     send_back(held)
-    act_stage(groups - 1)
     back_stage(groups - 1)
 
     for copies in (tok_copies, grad_copies):

time: 164 us -> 165 us (level)
  no operation moved by 1% of the time
where the time goes in v4:
time: 165 us; the launch traced here: 164 us
  Pallas kernels  128 us (78%)
  matrix products  25.7 us (16%)
  starting transfers between devices  8.05 us (5%)
    pallas_call x1, Pallas kernels, exchange(): pl.pallas_call(functools.partial(exchange_kernel, owners), out_shape=(wid...  128 us
    dot_general x3, matrix products, outer(): lax.dot_general(left, right, contract_rows, preferred_element_type=jnp.fl...  19.4 us
    ppermute x4, starting transfers between devices, fused_shards(): lax.ppermute(rows, 'expert', [(i, i ^ owners - GROUP + k) for i in range(...  8.05 us
  transfers between devices with their start and end apart: 4, of which 0 were waited for; matrix products, arithmetic and copies ran while one was open for 12% of the time, Pallas kernels for 0%

profile of v4, /device:TPU:0, one launch (start us, length us, event | category | flops | bytes accessed | tf_op | source)
XLA Modules:
  0.0 164.5 jit_solution(593610034148151677)
XLA Ops:
  0.6 0.0 copy-start
  0.6 0.0 copy-start.2
  0.7 0.8 copy.11
  1.5 0.2 convert_reduce_fusion
  1.7 0.8 fusion.16
  2.4 2.0 %convolution_convert_fusion.send_tokens = bf16[512,2048]{1,0:T(8,128)(2,1)} fusion(bf16[256,2048]{1,0:T(8,128)(2,1)S(1)} %copy-done, s32[256]{0:T(256)S(1)} %get-tuple-element.27, s32[256]{0:T(256)S(1)} %get-tuple-element.26), kind=kOutput, calls=%fused_computation.4 | convolution fusion | flops 538312704 | bytes 3147776 | tf_op jit(solution)/shard_map/dot_general | solution.py:416
  4.5 0.2 add_reduce_fusion
  4.7 2.0 %multiply_convert_fusion.send_grads = bf16[512,2048]{1,0:T(8,128)(2,1)} fusion(bf16[256,2048]{1,0:T(8,128)(2,1)S(1)} %copy-done.2, f32[512]{0:T(512)S(1)} %add_reduce_fusion, s32[256]{0:T(256)S(1)} %get-tuple-element.27, s32[256]{0:T(256)S(1)} %get-tuple-element.26), kind=kOutput, calls=%fused_computation.3 | convolution fusion | flops 539361280 | bytes 3149824 | tf_op jit(solution)/shard_map/dot_general | solution.py:418
  6.7 127.9 %exchange.1 = (bf16[512,2048]{1,0:T(8,128)(2,1)}, bf16[512,2048]{1,0:T(8,128)(2,1)}, bf16[512,1024]{1,0:T(8,128)(2,1)}, bf16[512,1024]{1,0:T(8,128)(2,1)}, bf16[...) custom-call(bf16[512,2048]{1,0:T(8,128)(2,1)} %convolution_convert_f, ...), custom_call_target="tpu_custom_call" | custom-call | flops 10737418240 | bytes 26214400 | tf_op jit(solution)/shard_map/exchange/pallas_call | solution.py:365
  134.6 2.3 %collective-permute-start = (bf16[32,2048]{1,0:T(8,128)(2,1)}, bf16[32,2048]{1,0:T(8,128)(2,1)S(1)}, u32[]{:S(2)}, u32[]{:S(2)}) collective-permute-start(bf16[32,2048]{1,0:T(8,128)(2,1)} %get-tuple-element.15), channel_id=1, source_target_pairs={{0,12},{1,13},{2,14},{3,15},{4,8},{5,9},{6,10},{7,11},{8,4},{9,5},... | collective-permute-start | bytes 393224 | tf_op jit(solution)/shard_map/ppermute | solution.py:426
  136.9 0.9 collective-permute-start.1
  137.8 3.3 %collective-permute-start.2 = (bf16[32,2048]{1,0:T(8,128)(2,1)}, bf16[32,2048]{1,0:T(8,128)(2,1)S(1)}, u32[]{:S(2)}, u32[]{:S(2)}) collective-permute-start(bf16[32,2048]{1,0:T(8,128)(2,1)} %get-tuple-element.17), channel_id=1, source_target_pairs={{0,14},{1,15},{2,12},{3,13},{4,10},{5,11},{6,8},{7,9},{8,6},{9,7},... | collective-permute-start | bytes 393224 | tf_op jit(solution)/shard_map/ppermute | solution.py:426
  141.1 1.5 collective-permute-start.3
  142.6 0.1 fusion.9
  142.8 7.8 %convolution_bitcast_fusion.2 = f32[1,2048,1024]{2,1,0:T(8,128)} fusion(bf16[512,2048]{1,0:T(8,128)(2,1)} %get-tuple-element.19, bf16[512,1024]{1,0:T(8,128)(2,1)} %get-tuple-element.20), kind=kOutput, calls=%fused_computation.2 | convolution fusion | flops 2147483648 | bytes 11534336 | tf_op jit(solution)/shard_map/dot_general | solution.py:431
  150.5 0.0 copy-done.3
  150.6 5.8 %convolution_bitcast_fusion.1 = f32[1,2048,1024]{2,1,0:T(8,128)} fusion(bf16[512,2048]{1,0:T(8,128)(2,1)S(1)} %copy-done.3, bf16[512,1024]{1,0:T(8,128)(2,1)S(1)} %copy-done.4), kind=kOutput, calls=%fused_computation.1 | convolution fusion | flops 2147483648 | bytes 11534336 | tf_op jit(solution)/shard_map/dot_general | solution.py:431
  156.4 5.8 %convolution_bitcast_fusion = f32[1,1024,2048]{2,1,0:T(8,128)} fusion(bf16[512,1024]{1,0:T(8,128)(2,1)S(1)} %copy-done.6, bf16[512,2048]{1,0:T(8,128)(2,1)S(1)} %copy-done.5), kind=kOutput, calls=%fused_computation | convolution fusion | flops 2147483648 | bytes 11534336 | tf_op jit(solution)/shard_map/dot_general | solution.py:431
  162.2 0.8 fusion.10
  163.0 0.0 collective-permute-done
  163.0 0.0 collective-permute-done.1
  163.0 0.0 collective-permute-done.2
  163.0 0.0 collective-permute-done.3
  163.0 1.5 fusion
  (13 shorter events, 0.0 us)
Async XLA Ops:
  0.6 1.8 %copy-start = (bf16[256,2048]{1,0:T(8,128)(2,1)S(1)}, bf16[256,2048]{1,0:T(8,128)(2,1)}, u32[]{:S(2)}) copy-start(bf16[256,2048]{1,0:T(8,128)(2,1)} %param.7) | copy-start | bytes 3145732
  0.6 4.0 %copy-start.2 = (bf16[256,2048]{1,0:T(8,128)(2,1)S(1)}, bf16[256,2048]{1,0:T(8,128)(2,1)}, u32[]{:S(2)}) copy-start(bf16[256,2048]{1,0:T(8,128)(2,1)} %param.8) | copy-start | bytes 3145732
  134.6 28.4 %collective-permute-start = (bf16[32,2048]{1,0:T(8,128)(2,1)}, bf16[32,2048]{1,0:T(8,128)(2,1)S(1)}, u32[]{:S(2)}, u32[]{:S(2)}) collective-permute-start(bf16[32,2048]{1,0:T(8,128)(2,1)} %get-tuple-element.15), channel_id=1, source_target_pairs={{0,12},{1,13},{2,14},{3,15},{4,8},{5,9},{6,10},{7,11},{8,4},{9,5},... | collective-permute-start | bytes 393224 | tf_op jit(solution)/shard_map/ppermute | solution.py:426
  136.9 26.1 %collective-permute-start.1 = (bf16[32,2048]{1,0:T(8,128)(2,1)}, bf16[32,2048]{1,0:T(8,128)(2,1)S(1)}, u32[]{:S(2)}, u32[]{:S(2)}) collective-permute-start(bf16[32,2048]{1,0:T(8,128)(2,1)} %get-tuple-element.16), channel_id=1, source_target_pairs={{0,13},{1,12},{2,15},{3,14},{4,9},{5,8},{6,11},{7,10},{8,5},{9,4},... | collective-permute-start | bytes 393224 | tf_op jit(solution)/shard_map/ppermute | solution.py:426
  137.8 25.1 %collective-permute-start.2 = (bf16[32,2048]{1,0:T(8,128)(2,1)}, bf16[32,2048]{1,0:T(8,128)(2,1)S(1)}, u32[]{:S(2)}, u32[]{:S(2)}) collective-permute-start(bf16[32,2048]{1,0:T(8,128)(2,1)} %get-tuple-element.17), channel_id=1, source_target_pairs={{0,14},{1,15},{2,12},{3,13},{4,10},{5,11},{6,8},{7,9},{8,6},{9,7},... | collective-permute-start | bytes 393224 | tf_op jit(solution)/shard_map/ppermute | solution.py:426
  141.1 21.9 %collective-permute-start.3 = (bf16[32,2048]{1,0:T(8,128)(2,1)}, bf16[32,2048]{1,0:T(8,128)(2,1)S(1)}, u32[]{:S(2)}, u32[]{:S(2)}) collective-permute-start(bf16[32,2048]{1,0:T(8,128)(2,1)} %get-tuple-element.18), channel_id=1, source_target_pairs={{0,15},{1,14},{2,13},{3,12},{4,11},{5,10},{6,9},{7,8},{8,7},{9,6},... | collective-permute-start | bytes 393224 | tf_op jit(solution)/shard_map/ppermute | solution.py:426
  142.7 7.8 %copy-start.3 = (bf16[512,2048]{1,0:T(8,128)(2,1)S(1)}, bf16[512,2048]{1,0:T(8,128)(2,1)}, u32[]{:S(2)}) copy-start(bf16[512,2048]{1,0:T(8,128)(2,1)} %get-tuple-element.19) | copy-start | bytes 6291460
  142.7 7.8 %copy-start.4 = (bf16[512,1024]{1,0:T(8,128)(2,1)S(1)}, bf16[512,1024]{1,0:T(8,128)(2,1)}, u32[]{:S(2)}) copy-start(bf16[512,1024]{1,0:T(8,128)(2,1)} %get-tuple-element.21) | copy-start | bytes 3145732
  150.5 5.8 %copy-start.5 = (bf16[512,2048]{1,0:T(8,128)(2,1)S(1)}, bf16[512,2048]{1,0:T(8,128)(2,1)}, u32[]{:S(2)}) copy-start(bf16[512,2048]{1,0:T(8,128)(2,1)} %get-tuple-element.23) | copy-start | bytes 6291460
  150.6 5.8 %copy-start.6 = (bf16[512,1024]{1,0:T(8,128)(2,1)S(1)}, bf16[512,1024]{1,0:T(8,128)(2,1)}, u32[]{:S(2)}) copy-start(bf16[512,1024]{1,0:T(8,128)(2,1)} %get-tuple-element.22) | copy-start | bytes 3145732
  156.4 5.8 %copy-start.1 = (bf16[384,2048]{1,0:T(8,128)(2,1)S(1)}, bf16[384,2048]{1,0:T(8,128)(2,1)}, u32[]{:S(2)}) copy-start(bf16[384,2048]{1,0:T(8,128)(2,1)} %get-tuple-element.14) | copy-start | bytes 4718596

commit v5 on v3

--- a/solution.py
+++ b/solution.py
@@ -226,6 +226,7 @@
             copies[far[i]].start()
             for k in near[2 * i : 2 * i + 2]:
                 copies[k].start()
+
     for first in range(GROUP, half, GROUP):
         for copies in (tok_copies, grad_copies):
             for k in far[first : first + GROUP]:
@@ -241,9 +242,10 @@
             else:
                 copies[k].wait_recv()
 
-    def pre_stage(g):
-        arrive(g, tok_copies, own[0])
-        rows = pl.ds(g * GROUP * MOST, GROUP * MOST)
+    def pre_stage(g, span=1):
+        for each in range(g, g + span):
+            arrive(each, tok_copies, own[0])
+        rows = pl.ds(g * GROUP * MOST, span * GROUP * MOST)
 
         @pl.loop(0, width // TILE)
         def _(c):
@@ -257,10 +259,13 @@
                 block, up_mat[:, cols], preferred_element_type=jnp.float32
             ).astype(jnp.bfloat16)
 
-        pre_copies[g].start()
-
-    def act_stage(g):
-        rows = pl.ds(g * GROUP * MOST, GROUP * MOST)
+        for each in range(g, g + span):
+            pre_copies[each].start()
+
+    def act_stage(g, span=1):
+        for each in range(g, g + span):
+            arrive(each, grad_copies, own[1])
+        rows = pl.ds(g * GROUP * MOST, span * GROUP * MOST)
 
         @pl.loop(0, width // TILE)
         def _(c):
@@ -272,12 +277,14 @@
                 preferred_element_type=jnp.float32,
             ).astype(jnp.bfloat16)
 
-        act_copies[g].start()
-
-    def back_stage(g):
-        pre_copies[g].wait_recv()
-        act_copies[g].wait_recv()
-        rows = pl.ds(g * GROUP * MOST, GROUP * MOST)
+        for each in range(g, g + span):
+            act_copies[each].start()
+
+    def back_stage(g, span=1):
+        for each in range(g, g + span):
+            pre_copies[each].wait_recv()
+            act_copies[each].wait_recv()
+        rows = pl.ds(g * GROUP * MOST, span * GROUP * MOST)
 
         @pl.loop(0, width // TILE)
         def _(c):
@@ -309,7 +316,7 @@
                 preferred_element_type=jnp.float32,
             )
             sums = sums.astype(jnp.bfloat16)
-            if g < groups - 1:
+            if g + span < groups:
                 slot_grad[rows, cols] = sums
             else:
                 for i in range(GROUP):
@@ -325,21 +332,18 @@
     for load in loads:
         load.wait()
     near_groups = groups // 2
-    for g in range(near_groups + 1):
-        pre_stage(g)
-    for g in range(near_groups + 1):
-        arrive(g, grad_copies, own[1])
-        act_stage(g)
+    pre_stage(0, near_groups)
+    pre_stage(near_groups)
+    act_stage(0, near_groups)
+    act_stage(near_groups)
+    back_stage(0, near_groups + 1)
     for g in range(near_groups):
-        back_stage(g)
         send_back(members(g))
-    back_stage(near_groups)
     held = members(near_groups)[GROUP // 2 :]
     send_back(members(near_groups)[: GROUP // 2])
     pre_stage(groups - 1)
-    arrive(groups - 1, grad_copies, own[1])
+    act_stage(groups - 1)
     send_back(held)
-    act_stage(groups - 1)
     back_stage(groups - 1)
 
     for copies in (tok_copies, grad_copies):

time: 164 us -> 163 us (level)
  no operation moved by 1% of the time
where the time goes in v5:
time: 163 us
  Pallas kernels  126 us (77%)
  matrix products  25.7 us (16%)
  starting transfers between devices  8.05 us (5%)
    pallas_call x1, Pallas kernels, exchange(): pl.pallas_call(functools.partial(exchange_kernel, owners), out_shape=(wid...  126 us
    dot_general x3, matrix products, outer(): lax.dot_general(left, right, contract_rows, preferred_element_type=jnp.fl...  19.4 us
    ppermute x4, starting transfers between devices, fused_shards(): lax.ppermute(rows, 'expert', [(i, i ^ owners - GROUP + k) for i in range(...  8.05 us
  transfers between devices with their start and end apart: 4, of which 0 were waited for; matrix products, arithmetic and copies ran while one was open for 12% of the time, Pallas kernels for 0%

profile of v5, /device:TPU:0, one launch (start us, length us, event | category | flops | bytes accessed | tf_op | source)
XLA Modules:
  0.0 162.8 jit_solution(7546106931454100659)
XLA Ops:
  0.6 0.0 copy-start
  0.7 0.8 copy.11
  1.5 0.2 convert_reduce_fusion
  1.7 0.8 fusion.16
  2.4 2.0 %convolution_convert_fusion.send_tokens = bf16[512,2048]{1,0:T(8,128)(2,1)} fusion(bf16[256,2048]{1,0:T(8,128)(2,1)S(1)} %copy-done, s32[256]{0:T(256)S(1)} %get-tuple-element.27, s32[256]{0:T(256)S(1)} %get-tuple-element.26), kind=kOutput, calls=%fused_computation.4 | convolution fusion | flops 538312704 | bytes 3147776 | tf_op jit(solution)/shard_map/dot_general | solution.py:420
  4.5 0.2 add_reduce_fusion
  4.7 0.0 copy-done.2
  4.7 2.0 %multiply_convert_fusion.send_grads = bf16[512,2048]{1,0:T(8,128)(2,1)} fusion(bf16[256,2048]{1,0:T(8,128)(2,1)S(1)} %copy-done.2, f32[512]{0:T(512)S(1)} %add_reduce_fusion, s32[256]{0:T(256)S(1)} %get-tuple-element.27, s32[256]{0:T(256)S(1)} %get-tuple-element.26), kind=kOutput, calls=%fused_computation.3 | convolution fusion | flops 539361280 | bytes 3149824 | tf_op jit(solution)/shard_map/dot_general | solution.py:422
  6.7 126.2 %exchange.1 = (bf16[512,2048]{1,0:T(8,128)(2,1)}, bf16[512,2048]{1,0:T(8,128)(2,1)}, bf16[512,1024]{1,0:T(8,128)(2,1)}, bf16[512,1024]{1,0:T(8,128)(2,1)}, bf16[...) custom-call(bf16[512,2048]{1,0:T(8,128)(2,1)} %convolution_convert_f, ...), custom_call_target="tpu_custom_call" | custom-call | flops 10737418240 | bytes 26214400 | tf_op jit(solution)/shard_map/exchange/pallas_call | solution.py:369
  132.9 0.7 collective-permute-start
  133.6 2.8 %collective-permute-start.1 = (bf16[32,2048]{1,0:T(8,128)(2,1)}, bf16[32,2048]{1,0:T(8,128)(2,1)S(1)}, u32[]{:S(2)}, u32[]{:S(2)}) collective-permute-start(bf16[32,2048]{1,0:T(8,128)(2,1)} %get-tuple-element.16), channel_id=1, source_target_pairs={{0,13},{1,12},{2,15},{3,14},{4,9},{5,8},{6,11},{7,10},{8,5},{9,4},... | collective-permute-start | bytes 393224 | tf_op jit(solution)/shard_map/ppermute | solution.py:430
  136.4 2.2 %collective-permute-start.2 = (bf16[32,2048]{1,0:T(8,128)(2,1)}, bf16[32,2048]{1,0:T(8,128)(2,1)S(1)}, u32[]{:S(2)}, u32[]{:S(2)}) collective-permute-start(bf16[32,2048]{1,0:T(8,128)(2,1)} %get-tuple-element.17), channel_id=1, source_target_pairs={{0,14},{1,15},{2,12},{3,13},{4,10},{5,11},{6,8},{7,9},{8,6},{9,7},... | collective-permute-start | bytes 393224 | tf_op jit(solution)/shard_map/ppermute | solution.py:430
  138.6 2.3 %collective-permute-start.3 = (bf16[32,2048]{1,0:T(8,128)(2,1)}, bf16[32,2048]{1,0:T(8,128)(2,1)S(1)}, u32[]{:S(2)}, u32[]{:S(2)}) collective-permute-start(bf16[32,2048]{1,0:T(8,128)(2,1)} %get-tuple-element.18), channel_id=1, source_target_pairs={{0,15},{1,14},{2,13},{3,12},{4,11},{5,10},{6,9},{7,8},{8,7},{9,6},... | collective-permute-start | bytes 393224 | tf_op jit(solution)/shard_map/ppermute | solution.py:430
  141.0 0.1 fusion.9
  141.1 0.0 copy-start.3
  141.1 7.8 %convolution_bitcast_fusion.2 = f32[1,2048,1024]{2,1,0:T(8,128)} fusion(bf16[512,2048]{1,0:T(8,128)(2,1)} %get-tuple-element.19, bf16[512,1024]{1,0:T(8,128)(2,1)} %get-tuple-element.20), kind=kOutput, calls=%fused_computation.2 | convolution fusion | flops 2147483648 | bytes 11534336 | tf_op jit(solution)/shard_map/dot_general | solution.py:435
  148.9 5.8 %convolution_bitcast_fusion.1 = f32[1,2048,1024]{2,1,0:T(8,128)} fusion(bf16[512,2048]{1,0:T(8,128)(2,1)S(1)} %copy-done.3, bf16[512,1024]{1,0:T(8,128)(2,1)S(1)} %copy-done.4), kind=kOutput, calls=%fused_computation.1 | convolution fusion | flops 2147483648 | bytes 11534336 | tf_op jit(solution)/shard_map/dot_general | solution.py:435
  154.7 5.8 %convolution_bitcast_fusion = f32[1,1024,2048]{2,1,0:T(8,128)} fusion(bf16[512,1024]{1,0:T(8,128)(2,1)S(1)} %copy-done.6, bf16[512,2048]{1,0:T(8,128)(2,1)S(1)} %copy-done.5), kind=kOutput, calls=%fused_computation | convolution fusion | flops 2147483648 | bytes 11534336 | tf_op jit(solution)/shard_map/dot_general | solution.py:435
  160.5 0.8 fusion.10
  161.3 0.0 collective-permute-done
  161.3 0.0 collective-permute-done.1
  161.3 0.0 collective-permute-done.2
  161.3 0.0 collective-permute-done.3
  161.3 1.5 fusion
  (13 shorter events, 0.0 us)
Async XLA Ops:
  0.6 1.8 %copy-start = (bf16[256,2048]{1,0:T(8,128)(2,1)S(1)}, bf16[256,2048]{1,0:T(8,128)(2,1)}, u32[]{:S(2)}) copy-start(bf16[256,2048]{1,0:T(8,128)(2,1)} %param.7) | copy-start | bytes 3145732
  0.6 4.0 %copy-start.2 = (bf16[256,2048]{1,0:T(8,128)(2,1)S(1)}, bf16[256,2048]{1,0:T(8,128)(2,1)}, u32[]{:S(2)}) copy-start(bf16[256,2048]{1,0:T(8,128)(2,1)} %param.8) | copy-start | bytes 3145732
  132.9 28.4 %collective-permute-start = (bf16[32,2048]{1,0:T(8,128)(2,1)}, bf16[32,2048]{1,0:T(8,128)(2,1)S(1)}, u32[]{:S(2)}, u32[]{:S(2)}) collective-permute-start(bf16[32,2048]{1,0:T(8,128)(2,1)} %get-tuple-element.15), channel_id=1, source_target_pairs={{0,12},{1,13},{2,14},{3,15},{4,8},{5,9},{6,10},{7,11},{8,4},{9,5},... | collective-permute-start | bytes 393224 | tf_op jit(solution)/shard_map/ppermute | solution.py:430
  133.6 27.7 %collective-permute-start.1 = (bf16[32,2048]{1,0:T(8,128)(2,1)}, bf16[32,2048]{1,0:T(8,128)(2,1)S(1)}, u32[]{:S(2)}, u32[]{:S(2)}) collective-permute-start(bf16[32,2048]{1,0:T(8,128)(2,1)} %get-tuple-element.16), channel_id=1, source_target_pairs={{0,13},{1,12},{2,15},{3,14},{4,9},{5,8},{6,11},{7,10},{8,5},{9,4},... | collective-permute-start | bytes 393224 | tf_op jit(solution)/shard_map/ppermute | solution.py:430
  136.4 24.9 %collective-permute-start.2 = (bf16[32,2048]{1,0:T(8,128)(2,1)}, bf16[32,2048]{1,0:T(8,128)(2,1)S(1)}, u32[]{:S(2)}, u32[]{:S(2)}) collective-permute-start(bf16[32,2048]{1,0:T(8,128)(2,1)} %get-tuple-element.17), channel_id=1, source_target_pairs={{0,14},{1,15},{2,12},{3,13},{4,10},{5,11},{6,8},{7,9},{8,6},{9,7},... | collective-permute-start | bytes 393224 | tf_op jit(solution)/shard_map/ppermute | solution.py:430
  138.6 22.7 %collective-permute-start.3 = (bf16[32,2048]{1,0:T(8,128)(2,1)}, bf16[32,2048]{1,0:T(8,128)(2,1)S(1)}, u32[]{:S(2)}, u32[]{:S(2)}) collective-permute-start(bf16[32,2048]{1,0:T(8,128)(2,1)} %get-tuple-element.18), channel_id=1, source_target_pairs={{0,15},{1,14},{2,13},{3,12},{4,11},{5,10},{6,9},{7,8},{8,7},{9,6},... | collective-permute-start | bytes 393224 | tf_op jit(solution)/shard_map/ppermute | solution.py:430
  141.1 7.8 %copy-start.3 = (bf16[512,2048]{1,0:T(8,128)(2,1)S(1)}, bf16[512,2048]{1,0:T(8,128)(2,1)}, u32[]{:S(2)}) copy-start(bf16[512,2048]{1,0:T(8,128)(2,1)} %get-tuple-element.19) | copy-start | bytes 6291460
  141.1 7.8 %copy-start.4 = (bf16[512,1024]{1,0:T(8,128)(2,1)S(1)}, bf16[512,1024]{1,0:T(8,128)(2,1)}, u32[]{:S(2)}) copy-start(bf16[512,1024]{1,0:T(8,128)(2,1)} %get-tuple-element.21) | copy-start | bytes 3145732
  148.9 5.8 %copy-start.5 = (bf16[512,2048]{1,0:T(8,128)(2,1)S(1)}, bf16[512,2048]{1,0:T(8,128)(2,1)}, u32[]{:S(2)}) copy-start(bf16[512,2048]{1,0:T(8,128)(2,1)} %get-tuple-element.23) | copy-start | bytes 6291460
  148.9 5.8 %copy-start.6 = (bf16[512,1024]{1,0:T(8,128)(2,1)S(1)}, bf16[512,1024]{1,0:T(8,128)(2,1)}, u32[]{:S(2)}) copy-start(bf16[512,1024]{1,0:T(8,128)(2,1)} %get-tuple-element.22) | copy-start | bytes 3145732
  154.7 5.8 %copy-start.1 = (bf16[384,2048]{1,0:T(8,128)(2,1)S(1)}, bf16[384,2048]{1,0:T(8,128)(2,1)}, u32[]{:S(2)}) copy-start(bf16[384,2048]{1,0:T(8,128)(2,1)} %get-tuple-element.14) | copy-start | bytes 4718596
